TPU v7x, 512 devices: a whole 4x4x16 slice. The times are simulated.
512 devices in a mesh: section: 16 (over y, x), tensor: 32 (over z, core).
Axes of the slice: x: 4, y: 4, z: 16, core: 2. Of those that a mesh axis runs over, the one named last changes fastest.
Arguments:
- section_inputs: bfloat16 [16, 2, 128, 8192], P('section', None, None, 'tensor'), may hold values from -6 to 6
- out_grad: bfloat16 [2, 128, 8192], P(None, None, 'tensor'), may hold values from -6 to 6
- w1: bfloat16 [16, 64, 128, 128], P('section', 'tensor'), may hold values from -0.5 to 0.5
- w2: bfloat16 [16, 64, 128, 512], P('section', 'tensor'), may hold values from -0.5 to 0.5
- w3: bfloat16 [16, 64, 512, 128], P('section', 'tensor'), may hold values from -0.25 to 0.25
- w4: bfloat16 [16, 64, 128, 128], P('section', 'tensor'), may hold values from -0.25 to 0.25
Outputs:
- grad_inputs: bfloat16 [16, 2, 128, 8192], P('section', None, None, 'tensor')
- grad_w1: float32 [16, 64, 128, 128], P('section', 'tensor')
- grad_w2: float32 [16, 64, 128, 512], P('section', 'tensor')
- grad_w3: float32 [16, 64, 512, 128], P('section', 'tensor')
- grad_w4: float32 [16, 64, 128, 128], P('section', 'tensor')
All inputs are finite; a program needn't handle non-finite values.
Results may differ from a plain program's by a relative error of at most 0.035.
Values may be sent and summed in bfloat16 or wider, within the bound.
No kernel may reach another device: no remote copies, remote signals or barrier semaphores. Data moves between devices by JAX's collectives and lax.ppermute only.
A program may use at most 64 MiB of HBM per device.

v0:
```python
import jax
import jax.numpy as jnp
from jax import lax
from jax.sharding import PartitionSpec as P

SQRT_TWO_PI = 0.7978845608028654
CUBIC_TERM = 0.044715


def passed_along(value, axis, steps):
    count = lax.axis_size(axis)
    leading, last = (max(0, -steps), min(count, count - steps))
    return lax.ppermute(value, axis, [(source, source + steps) for source in range(leading, last)])


def gelu_tanh(linear):
    inner = SQRT_TWO_PI * (linear + CUBIC_TERM * linear * linear * linear)
    return 0.5 * linear * (1.0 + jnp.tanh(inner))


def gelu_slope(linear):
    inner = SQRT_TWO_PI * (linear + CUBIC_TERM * linear * linear * linear)
    tangent = jnp.tanh(inner)
    return 0.5 * (1.0 + tangent) + 0.5 * linear * (1.0 - tangent * tangent) * SQRT_TWO_PI * (
        1.0 + 3.0 * CUBIC_TERM * linear * linear
    )


def matrix_product(form, left_side, right_side):
    return jnp.einsum(form, left_side, right_side, preferred_element_type=jnp.float32)


def local(section_inputs, out_grad, w1, w2, w3, w4):
    tensor_size = lax.axis_size("tensor")
    section_count = lax.axis_size("section")
    section_id = lax.axis_index("section")
    micro_count = section_inputs.shape[1]
    tok_rows = section_inputs.shape[2]
    local_factor = w1.shape[1]
    block_width = w1.shape[2]
    b_local = w2.shape[1]
    hidden_width = w2.shape[3]
    count_of_blocks = local_factor * tensor_size
    spread_rows = block_width // count_of_blocks
    all_rows = micro_count * tok_rows
    input_rows = section_inputs[0].reshape(all_rows, local_factor, block_width)
    targets = out_grad.reshape(all_rows, local_factor, block_width)
    leading_weight = w1[0]
    w_second = w2[0].reshape(b_local, count_of_blocks, spread_rows, hidden_width)
    w_third = w3[0]
    closing_weight = w4[0].reshape(local_factor, count_of_blocks, spread_rows, block_width)
    raised_rows = matrix_product("owz,wzy->wyo", input_rows, leading_weight).astype(jnp.bfloat16)
    mixed = lax.all_to_all(raised_rows, "tensor", split_axis=1, concat_axis=0, tiled=True)
    number_of_items = mixed.shape[2]
    linear = matrix_product(
        "abrt,barn->bnt",
        mixed.reshape(count_of_blocks, b_local, spread_rows, number_of_items),
        w_second,
    )
    gelu_out = gelu_tanh(linear).astype(jnp.bfloat16)
    lowered = matrix_product("bnt,bnk->bkt", gelu_out, w_third).astype(jnp.bfloat16)
    handed_back = lax.all_to_all(lowered, "tensor", split_axis=1, concat_axis=0, tiled=True)

    def weight_terms(
        input_matrix_rows,
        mix_rows,
        gelu_rows,
        return_rows,
        outgoing_gradient,
        grad_mid,
        grad_lin,
        gradient_returned,
    ):
        number_of_items = input_matrix_rows.shape[0]
        grad_fourth = matrix_product(
            "nxpq,qxf->xnpf",
            return_rows.reshape(count_of_blocks, local_factor, spread_rows, number_of_items),
            outgoing_gradient,
        ).reshape(local_factor, block_width, block_width)
        grad_third = matrix_product("bnt,bkt->bnk", gelu_rows, grad_mid)
        grad_second = matrix_product(
            "abrt,bnt->barn",
            mix_rows.reshape(count_of_blocks, b_local, spread_rows, number_of_items),
            grad_lin,
        ).reshape(b_local, block_width, hidden_width)
        leading_gradient = matrix_product("qln,lvq->lnv", input_matrix_rows, gradient_returned)
        return (leading_gradient, grad_second, grad_third, grad_fourth)

    def one_step(step_index, received, collected):
        step_lag = step_index - (section_count - 1 - section_id)
        active = step_lag == 0
        outgoing_gradient = jnp.where(section_id == section_count - 1, targets, received)
        lower_gradient = matrix_product("zqs,qhis->hqiz", outgoing_gradient, closing_weight).astype(
            jnp.bfloat16
        )
        lower_gradient = lower_gradient.reshape(
            count_of_blocks, local_factor * spread_rows, all_rows
        )
        grad_mid = lax.all_to_all(lower_gradient, "tensor", split_axis=0, concat_axis=1, tiled=True)
        grad_hid = matrix_product("bkt,bnk->bnt", grad_mid, w_third)
        grad_lin = (grad_hid * gelu_slope(linear)).astype(jnp.bfloat16)
        grad_up = matrix_product("bnt,barn->abrt", grad_lin, w_second).astype(jnp.bfloat16)
        grad_up = grad_up.reshape(count_of_blocks, b_local * spread_rows, all_rows)
        gradient_returned = lax.all_to_all(
            grad_up, "tensor", split_axis=0, concat_axis=1, tiled=True
        )
        incoming_gradient = (
            outgoing_gradient.astype(jnp.float32)
            + matrix_product("vip,vwi->pvw", gradient_returned, leading_weight)
        ).astype(jnp.bfloat16)
        grads_in, kept = collected
        old_rows = grads_in
        grads_in = jnp.where(active, incoming_gradient, old_rows)
        terms = weight_terms(
            input_rows,
            mixed,
            gelu_out,
            handed_back,
            outgoing_gradient,
            grad_mid,
            grad_lin,
            gradient_returned,
        )
        kept = tuple((total + jnp.where(active, term, 0.0) for total, term in zip(kept, terms)))
        return (incoming_gradient, (grads_in, kept))

    grads_start = jnp.zeros((all_rows, local_factor, block_width), jnp.bfloat16)
    kept_start = (
        jnp.zeros((local_factor, block_width, block_width), jnp.float32),
        jnp.zeros((b_local, block_width, hidden_width), jnp.float32),
        jnp.zeros((b_local, hidden_width, block_width), jnp.float32),
        jnp.zeros((local_factor, block_width, block_width), jnp.float32),
    )

    def loop_body(step_index, carried):
        received, collected = carried
        incoming_gradient, collected = one_step(step_index, received, collected)
        received = passed_along(incoming_gradient, "section", -1)
        return (received, collected)

    received_start = jnp.zeros((all_rows, local_factor, block_width), jnp.bfloat16)
    received, collected = lax.fori_loop(
        0, section_count - 1, loop_body, (received_start, (grads_start, kept_start))
    )
    last_grad, collected = one_step(section_count - 1, received, collected)
    grads_in, kept = collected
    grad_inputs = grads_in.reshape(1, micro_count, tok_rows, local_factor * block_width)
    return (grad_inputs, kept[0][None], kept[1][None], kept[2][None], kept[3][None])


def solution(mesh):
    in_specs = (
        P("section", None, None, "tensor"),
        P(None, None, "tensor"),
        P("section", "tensor", None, None),
        P("section", "tensor", None, None),
        P("section", "tensor", None, None),
        P("section", "tensor", None, None),
    )
    out_specs = (
        P("section", None, None, "tensor"),
        P("section", "tensor", None, None),
        P("section", "tensor", None, None),
        P("section", "tensor", None, None),
        P("section", "tensor", None, None),
    )
    return jax.shard_map(local, mesh=mesh, in_specs=in_specs, out_specs=out_specs, check_vma=False)
```

profile of v0, /device:TPU:1, one launch (start us, length us, event | category | flops | bytes accessed | tf_op | source)
XLA Modules:
  0.0 998.3 jit_solution(15184172093774898701)
XLA Ops:
  3.5 16.7 %all-to-all-start.2 = ((bf16[2,128,256]{2,0,1:T(2,128)(2,1)}), bf16[2,128,256]{2,0,1:T(2,128)(2,1)S(1)}, u32[]{:S(2)}, u32[]{:S(2)}) async-start(bf16[2,128,256]{2,0,1:T(2,128)(2,1)} %copy.132), calls=%async_computation.2 | async-start | bytes 262144 | tf_op jit(solution)/shard_map/all_to_all | solution.py:53
  20.6 15.5 %all-to-all-done.2 = bf16[2,128,256]{2,0,1:T(2,128)(2,1)S(1)} async-done(((bf16[2,128,256]{2,0,1:T(2,128)(2,1)}), bf16[2,128,256]{2,0,1:T(2,128)(2,1)S(1)}, u32[]{:S(2)}, u32[]{:S(2)}) %all-to-all-start.2) | async-done | bytes 131104 | tf_op jit(solution)/shard_map/all_to_all | solution.py:53
  60.8 884.2 %while.26 = (s32[]{:T(128)}, bf16[256,2,128]{2,0,1:T(8,128)(2,1)S(1)}, bf16[256,2,128]{2,0,1:T(8,128)(2,1)}, f32[2,128,128]{1,2,0:T(8,128)}, f32[2,128,512]{2,0,...) while((s32[]{:T(128)}, ...), condition=%wide.region_1.2_spmd.clone, body=%wide.region_0.1_spmd.clone.sunk | while | flops 342032384 | bytes 19530348 | solution.py:142
  68.5 15.8 %all-to-all-done = bf16[64,4,256]{2,1,0:T(4,128)(2,1)S(1)} async-done(((bf16[64,4,256]{2,1,0:T(4,128)(2,1)}), bf16[64,4,256]{2,1,0:T(4,128)(2,1)S(1)}, u32[]{:S(2)}, u32[]{:S(2)}) %all-to-all-start) | async-done | bytes 131104 | tf_op jit(solution)/shard_map/while/body/eval_jaxpr/all_to_all | solution.py:99
  94.4 14.9 %all-to-all-done.1 = bf16[64,4,256]{2,1,0:T(4,128)(2,1)S(1)} async-done(((bf16[64,4,256]{2,1,0:T(4,128)(2,1)}), bf16[64,4,256]{2,1,0:T(4,128)(2,1)S(1)}, u32[]{:S(2)}, u32[]{:S(2)}) %all-to-all-start.1) | async-done | bytes 131104 | tf_op jit(solution)/shard_map/while/body/eval_jaxpr/all_to_all | solution.py:104
  126.0 15.8 %all-to-all-done = bf16[64,4,256]{2,1,0:T(4,128)(2,1)S(1)} async-done(((bf16[64,4,256]{2,1,0:T(4,128)(2,1)}), bf16[64,4,256]{2,1,0:T(4,128)(2,1)S(1)}, u32[]{:S(2)}, u32[]{:S(2)}) %all-to-all-start) | async-done | bytes 131104 | tf_op jit(solution)/shard_map/while/body/eval_jaxpr/all_to_all | solution.py:99
  151.9 14.9 %all-to-all-done.1 = bf16[64,4,256]{2,1,0:T(4,128)(2,1)S(1)} async-done(((bf16[64,4,256]{2,1,0:T(4,128)(2,1)}), bf16[64,4,256]{2,1,0:T(4,128)(2,1)S(1)}, u32[]{:S(2)}, u32[]{:S(2)}) %all-to-all-start.1) | async-done | bytes 131104 | tf_op jit(solution)/shard_map/while/body/eval_jaxpr/all_to_all | solution.py:104
  183.4 15.8 %all-to-all-done = bf16[64,4,256]{2,1,0:T(4,128)(2,1)S(1)} async-done(((bf16[64,4,256]{2,1,0:T(4,128)(2,1)}), bf16[64,4,256]{2,1,0:T(4,128)(2,1)S(1)}, u32[]{:S(2)}, u32[]{:S(2)}) %all-to-all-start) | async-done | bytes 131104 | tf_op jit(solution)/shard_map/while/body/eval_jaxpr/all_to_all | solution.py:99
  209.3 14.9 %all-to-all-done.1 = bf16[64,4,256]{2,1,0:T(4,128)(2,1)S(1)} async-done(((bf16[64,4,256]{2,1,0:T(4,128)(2,1)}), bf16[64,4,256]{2,1,0:T(4,128)(2,1)S(1)}, u32[]{:S(2)}, u32[]{:S(2)}) %all-to-all-start.1) | async-done | bytes 131104 | tf_op jit(solution)/shard_map/while/body/eval_jaxpr/all_to_all | solution.py:104
  240.9 15.8 %all-to-all-done = bf16[64,4,256]{2,1,0:T(4,128)(2,1)S(1)} async-done(((bf16[64,4,256]{2,1,0:T(4,128)(2,1)}), bf16[64,4,256]{2,1,0:T(4,128)(2,1)S(1)}, u32[]{:S(2)}, u32[]{:S(2)}) %all-to-all-start) | async-done | bytes 131104 | tf_op jit(solution)/shard_map/while/body/eval_jaxpr/all_to_all | solution.py:99
  266.8 14.9 %all-to-all-done.1 = bf16[64,4,256]{2,1,0:T(4,128)(2,1)S(1)} async-done(((bf16[64,4,256]{2,1,0:T(4,128)(2,1)}), bf16[64,4,256]{2,1,0:T(4,128)(2,1)S(1)}, u32[]{:S(2)}, u32[]{:S(2)}) %all-to-all-start.1) | async-done | bytes 131104 | tf_op jit(solution)/shard_map/while/body/eval_jaxpr/all_to_all | solution.py:104
  298.6 15.8 %all-to-all-done = bf16[64,4,256]{2,1,0:T(4,128)(2,1)S(1)} async-done(((bf16[64,4,256]{2,1,0:T(4,128)(2,1)}), bf16[64,4,256]{2,1,0:T(4,128)(2,1)S(1)}, u32[]{:S(2)}, u32[]{:S(2)}) %all-to-all-start) | async-done | bytes 131104 | tf_op jit(solution)/shard_map/while/body/eval_jaxpr/all_to_all | solution.py:99
  324.5 14.9 %all-to-all-done.1 = bf16[64,4,256]{2,1,0:T(4,128)(2,1)S(1)} async-done(((bf16[64,4,256]{2,1,0:T(4,128)(2,1)}), bf16[64,4,256]{2,1,0:T(4,128)(2,1)S(1)}, u32[]{:S(2)}, u32[]{:S(2)}) %all-to-all-start.1) | async-done | bytes 131104 | tf_op jit(solution)/shard_map/while/body/eval_jaxpr/all_to_all | solution.py:104
  358.1 15.8 %all-to-all-done = bf16[64,4,256]{2,1,0:T(4,128)(2,1)S(1)} async-done(((bf16[64,4,256]{2,1,0:T(4,128)(2,1)}), bf16[64,4,256]{2,1,0:T(4,128)(2,1)S(1)}, u32[]{:S(2)}, u32[]{:S(2)}) %all-to-all-start) | async-done | bytes 131104 | tf_op jit(solution)/shard_map/while/body/eval_jaxpr/all_to_all | solution.py:99
  384.0 14.9 %all-to-all-done.1 = bf16[64,4,256]{2,1,0:T(4,128)(2,1)S(1)} async-done(((bf16[64,4,256]{2,1,0:T(4,128)(2,1)}), bf16[64,4,256]{2,1,0:T(4,128)(2,1)S(1)}, u32[]{:S(2)}, u32[]{:S(2)}) %all-to-all-start.1) | async-done | bytes 131104 | tf_op jit(solution)/shard_map/while/body/eval_jaxpr/all_to_all | solution.py:104
  417.7 15.8 %all-to-all-done = bf16[64,4,256]{2,1,0:T(4,128)(2,1)S(1)} async-done(((bf16[64,4,256]{2,1,0:T(4,128)(2,1)}), bf16[64,4,256]{2,1,0:T(4,128)(2,1)S(1)}, u32[]{:S(2)}, u32[]{:S(2)}) %all-to-all-start) | async-done | bytes 131104 | tf_op jit(solution)/shard_map/while/body/eval_jaxpr/all_to_all | solution.py:99
  443.6 14.9 %all-to-all-done.1 = bf16[64,4,256]{2,1,0:T(4,128)(2,1)S(1)} async-done(((bf16[64,4,256]{2,1,0:T(4,128)(2,1)}), bf16[64,4,256]{2,1,0:T(4,128)(2,1)S(1)}, u32[]{:S(2)}, u32[]{:S(2)}) %all-to-all-start.1) | async-done | bytes 131104 | tf_op jit(solution)/shard_map/while/body/eval_jaxpr/all_to_all | solution.py:104
  477.2 15.8 %all-to-all-done = bf16[64,4,256]{2,1,0:T(4,128)(2,1)S(1)} async-done(((bf16[64,4,256]{2,1,0:T(4,128)(2,1)}), bf16[64,4,256]{2,1,0:T(4,128)(2,1)S(1)}, u32[]{:S(2)}, u32[]{:S(2)}) %all-to-all-start) | async-done | bytes 131104 | tf_op jit(solution)/shard_map/while/body/eval_jaxpr/all_to_all | solution.py:99
  503.1 14.9 %all-to-all-done.1 = bf16[64,4,256]{2,1,0:T(4,128)(2,1)S(1)} async-done(((bf16[64,4,256]{2,1,0:T(4,128)(2,1)}), bf16[64,4,256]{2,1,0:T(4,128)(2,1)S(1)}, u32[]{:S(2)}, u32[]{:S(2)}) %all-to-all-start.1) | async-done | bytes 131104 | tf_op jit(solution)/shard_map/while/body/eval_jaxpr/all_to_all | solution.py:104
  536.8 15.8 %all-to-all-done = bf16[64,4,256]{2,1,0:T(4,128)(2,1)S(1)} async-done(((bf16[64,4,256]{2,1,0:T(4,128)(2,1)}), bf16[64,4,256]{2,1,0:T(4,128)(2,1)S(1)}, u32[]{:S(2)}, u32[]{:S(2)}) %all-to-all-start) | async-done | bytes 131104 | tf_op jit(solution)/shard_map/while/body/eval_jaxpr/all_to_all | solution.py:99
  562.7 14.9 %all-to-all-done.1 = bf16[64,4,256]{2,1,0:T(4,128)(2,1)S(1)} async-done(((bf16[64,4,256]{2,1,0:T(4,128)(2,1)}), bf16[64,4,256]{2,1,0:T(4,128)(2,1)S(1)}, u32[]{:S(2)}, u32[]{:S(2)}) %all-to-all-start.1) | async-done | bytes 131104 | tf_op jit(solution)/shard_map/while/body/eval_jaxpr/all_to_all | solution.py:104
  596.3 15.8 %all-to-all-done = bf16[64,4,256]{2,1,0:T(4,128)(2,1)S(1)} async-done(((bf16[64,4,256]{2,1,0:T(4,128)(2,1)}), bf16[64,4,256]{2,1,0:T(4,128)(2,1)S(1)}, u32[]{:S(2)}, u32[]{:S(2)}) %all-to-all-start) | async-done | bytes 131104 | tf_op jit(solution)/shard_map/while/body/eval_jaxpr/all_to_all | solution.py:99
  622.2 14.9 %all-to-all-done.1 = bf16[64,4,256]{2,1,0:T(4,128)(2,1)S(1)} async-done(((bf16[64,4,256]{2,1,0:T(4,128)(2,1)}), bf16[64,4,256]{2,1,0:T(4,128)(2,1)S(1)}, u32[]{:S(2)}, u32[]{:S(2)}) %all-to-all-start.1) | async-done | bytes 131104 | tf_op jit(solution)/shard_map/while/body/eval_jaxpr/all_to_all | solution.py:104
  655.9 15.8 %all-to-all-done = bf16[64,4,256]{2,1,0:T(4,128)(2,1)S(1)} async-done(((bf16[64,4,256]{2,1,0:T(4,128)(2,1)}), bf16[64,4,256]{2,1,0:T(4,128)(2,1)S(1)}, u32[]{:S(2)}, u32[]{:S(2)}) %all-to-all-start) | async-done | bytes 131104 | tf_op jit(solution)/shard_map/while/body/eval_jaxpr/all_to_all | solution.py:99
  681.8 14.9 %all-to-all-done.1 = bf16[64,4,256]{2,1,0:T(4,128)(2,1)S(1)} async-done(((bf16[64,4,256]{2,1,0:T(4,128)(2,1)}), bf16[64,4,256]{2,1,0:T(4,128)(2,1)S(1)}, u32[]{:S(2)}, u32[]{:S(2)}) %all-to-all-start.1) | async-done | bytes 131104 | tf_op jit(solution)/shard_map/while/body/eval_jaxpr/all_to_all | solution.py:104
  715.4 15.8 %all-to-all-done = bf16[64,4,256]{2,1,0:T(4,128)(2,1)S(1)} async-done(((bf16[64,4,256]{2,1,0:T(4,128)(2,1)}), bf16[64,4,256]{2,1,0:T(4,128)(2,1)S(1)}, u32[]{:S(2)}, u32[]{:S(2)}) %all-to-all-start) | async-done | bytes 131104 | tf_op jit(solution)/shard_map/while/body/eval_jaxpr/all_to_all | solution.py:99
  741.3 14.9 %all-to-all-done.1 = bf16[64,4,256]{2,1,0:T(4,128)(2,1)S(1)} async-done(((bf16[64,4,256]{2,1,0:T(4,128)(2,1)}), bf16[64,4,256]{2,1,0:T(4,128)(2,1)S(1)}, u32[]{:S(2)}, u32[]{:S(2)}) %all-to-all-start.1) | async-done | bytes 131104 | tf_op jit(solution)/shard_map/while/body/eval_jaxpr/all_to_all | solution.py:104
  775.0 15.8 %all-to-all-done = bf16[64,4,256]{2,1,0:T(4,128)(2,1)S(1)} async-done(((bf16[64,4,256]{2,1,0:T(4,128)(2,1)}), bf16[64,4,256]{2,1,0:T(4,128)(2,1)S(1)}, u32[]{:S(2)}, u32[]{:S(2)}) %all-to-all-start) | async-done | bytes 131104 | tf_op jit(solution)/shard_map/while/body/eval_jaxpr/all_to_all | solution.py:99
  800.9 14.9 %all-to-all-done.1 = bf16[64,4,256]{2,1,0:T(4,128)(2,1)S(1)} async-done(((bf16[64,4,256]{2,1,0:T(4,128)(2,1)}), bf16[64,4,256]{2,1,0:T(4,128)(2,1)S(1)}, u32[]{:S(2)}, u32[]{:S(2)}) %all-to-all-start.1) | async-done | bytes 131104 | tf_op jit(solution)/shard_map/while/body/eval_jaxpr/all_to_all | solution.py:104
  834.6 15.8 %all-to-all-done = bf16[64,4,256]{2,1,0:T(4,128)(2,1)S(1)} async-done(((bf16[64,4,256]{2,1,0:T(4,128)(2,1)}), bf16[64,4,256]{2,1,0:T(4,128)(2,1)S(1)}, u32[]{:S(2)}, u32[]{:S(2)}) %all-to-all-start) | async-done | bytes 131104 | tf_op jit(solution)/shard_map/while/body/eval_jaxpr/all_to_all | solution.py:99
  860.4 14.9 %all-to-all-done.1 = bf16[64,4,256]{2,1,0:T(4,128)(2,1)S(1)} async-done(((bf16[64,4,256]{2,1,0:T(4,128)(2,1)}), bf16[64,4,256]{2,1,0:T(4,128)(2,1)S(1)}, u32[]{:S(2)}, u32[]{:S(2)}) %all-to-all-start.1) | async-done | bytes 131104 | tf_op jit(solution)/shard_map/while/body/eval_jaxpr/all_to_all | solution.py:104
  894.1 15.8 %all-to-all-done = bf16[64,4,256]{2,1,0:T(4,128)(2,1)S(1)} async-done(((bf16[64,4,256]{2,1,0:T(4,128)(2,1)}), bf16[64,4,256]{2,1,0:T(4,128)(2,1)S(1)}, u32[]{:S(2)}, u32[]{:S(2)}) %all-to-all-start) | async-done | bytes 131104 | tf_op jit(solution)/shard_map/while/body/eval_jaxpr/all_to_all | solution.py:99
  (702 shorter events, 516.1 us)
Async XLA Ops:
  3.5 32.6 %all-to-all-start.2 = ((bf16[2,128,256]{2,0,1:T(2,128)(2,1)}), bf16[2,128,256]{2,0,1:T(2,128)(2,1)S(1)}, u32[]{:S(2)}, u32[]{:S(2)}) async-start(bf16[2,128,256]{2,0,1:T(2,128)(2,1)} %copy.132), calls=%async_computation.2 | async-start | bytes 262144 | tf_op jit(solution)/shard_map/all_to_all | solution.py:53
  38.8 21.3 %all-to-all-start.3 = ((bf16[2,128,256]{2,0,1:T(2,128)(2,1)}), bf16[2,128,256]{2,0,1:T(2,128)(2,1)S(1)}, u32[]{:S(2)}, u32[]{:S(2)}) async-start(bf16[2,128,256]{2,0,1:T(2,128)(2,1)} %copy.136), calls=%async_computation.3 | async-start | bytes 262144 | tf_op jit(solution)/shard_map/all_to_all | solution.py:62
  63.3 21.0 %all-to-all-start = ((bf16[64,4,256]{2,1,0:T(4,128)(2,1)}), bf16[64,4,256]{2,1,0:T(4,128)(2,1)S(1)}, u32[]{:S(2)}, u32[]{:S(2)}) async-start(bf16[64,4,256]{2,1,0:T(4,128)(2,1)} %copy.230), calls=%async_computation | async-start | bytes 262144 | tf_op jit(solution)/shard_map/while/body/eval_jaxpr/all_to_all | solution.py:99
  88.2 21.1 %all-to-all-start.1 = ((bf16[64,4,256]{2,1,0:T(4,128)(2,1)}), bf16[64,4,256]{2,1,0:T(4,128)(2,1)S(1)}, u32[]{:S(2)}, u32[]{:S(2)}) async-start(bf16[64,4,256]{2,1,0:T(4,128)(2,1)} %copy.232), calls=%async_computation.1 | async-start | bytes 262144 | tf_op jit(solution)/shard_map/while/body/eval_jaxpr/all_to_all | solution.py:104
  119.6 22.2 %all-to-all-start = ((bf16[64,4,256]{2,1,0:T(4,128)(2,1)}), bf16[64,4,256]{2,1,0:T(4,128)(2,1)S(1)}, u32[]{:S(2)}, u32[]{:S(2)}) async-start(bf16[64,4,256]{2,1,0:T(4,128)(2,1)} %copy.230), calls=%async_computation | async-start | bytes 262144 | tf_op jit(solution)/shard_map/while/body/eval_jaxpr/all_to_all | solution.py:99
  145.7 21.0 %all-to-all-start.1 = ((bf16[64,4,256]{2,1,0:T(4,128)(2,1)}), bf16[64,4,256]{2,1,0:T(4,128)(2,1)S(1)}, u32[]{:S(2)}, u32[]{:S(2)}) async-start(bf16[64,4,256]{2,1,0:T(4,128)(2,1)} %copy.232), calls=%async_computation.1 | async-start | bytes 262144 | tf_op jit(solution)/shard_map/while/body/eval_jaxpr/all_to_all | solution.py:104
  177.0 22.2 %all-to-all-start = ((bf16[64,4,256]{2,1,0:T(4,128)(2,1)}), bf16[64,4,256]{2,1,0:T(4,128)(2,1)S(1)}, u32[]{:S(2)}, u32[]{:S(2)}) async-start(bf16[64,4,256]{2,1,0:T(4,128)(2,1)} %copy.230), calls=%async_computation | async-start | bytes 262144 | tf_op jit(solution)/shard_map/while/body/eval_jaxpr/all_to_all | solution.py:99
  203.1 21.0 %all-to-all-start.1 = ((bf16[64,4,256]{2,1,0:T(4,128)(2,1)}), bf16[64,4,256]{2,1,0:T(4,128)(2,1)S(1)}, u32[]{:S(2)}, u32[]{:S(2)}) async-start(bf16[64,4,256]{2,1,0:T(4,128)(2,1)} %copy.232), calls=%async_computation.1 | async-start | bytes 262144 | tf_op jit(solution)/shard_map/while/body/eval_jaxpr/all_to_all | solution.py:104
  234.5 22.2 %all-to-all-start = ((bf16[64,4,256]{2,1,0:T(4,128)(2,1)}), bf16[64,4,256]{2,1,0:T(4,128)(2,1)S(1)}, u32[]{:S(2)}, u32[]{:S(2)}) async-start(bf16[64,4,256]{2,1,0:T(4,128)(2,1)} %copy.230), calls=%async_computation | async-start | bytes 262144 | tf_op jit(solution)/shard_map/while/body/eval_jaxpr/all_to_all | solution.py:99
  260.6 21.0 %all-to-all-start.1 = ((bf16[64,4,256]{2,1,0:T(4,128)(2,1)}), bf16[64,4,256]{2,1,0:T(4,128)(2,1)S(1)}, u32[]{:S(2)}, u32[]{:S(2)}) async-start(bf16[64,4,256]{2,1,0:T(4,128)(2,1)} %copy.232), calls=%async_computation.1 | async-start | bytes 262144 | tf_op jit(solution)/shard_map/while/body/eval_jaxpr/all_to_all | solution.py:104
  292.5 21.9 %all-to-all-start = ((bf16[64,4,256]{2,1,0:T(4,128)(2,1)}), bf16[64,4,256]{2,1,0:T(4,128)(2,1)S(1)}, u32[]{:S(2)}, u32[]{:S(2)}) async-start(bf16[64,4,256]{2,1,0:T(4,128)(2,1)} %copy.230), calls=%async_computation | async-start | bytes 262144 | tf_op jit(solution)/shard_map/while/body/eval_jaxpr/all_to_all | solution.py:99
  318.3 21.0 %all-to-all-start.1 = ((bf16[64,4,256]{2,1,0:T(4,128)(2,1)}), bf16[64,4,256]{2,1,0:T(4,128)(2,1)S(1)}, u32[]{:S(2)}, u32[]{:S(2)}) async-start(bf16[64,4,256]{2,1,0:T(4,128)(2,1)} %copy.232), calls=%async_computation.1 | async-start | bytes 262144 | tf_op jit(solution)/shard_map/while/body/eval_jaxpr/all_to_all | solution.py:104
  352.0 21.9 %all-to-all-start = ((bf16[64,4,256]{2,1,0:T(4,128)(2,1)}), bf16[64,4,256]{2,1,0:T(4,128)(2,1)S(1)}, u32[]{:S(2)}, u32[]{:S(2)}) async-start(bf16[64,4,256]{2,1,0:T(4,128)(2,1)} %copy.230), calls=%async_computation | async-start | bytes 262144 | tf_op jit(solution)/shard_map/while/body/eval_jaxpr/all_to_all | solution.py:99
  377.8 21.0 %all-to-all-start.1 = ((bf16[64,4,256]{2,1,0:T(4,128)(2,1)}), bf16[64,4,256]{2,1,0:T(4,128)(2,1)S(1)}, u32[]{:S(2)}, u32[]{:S(2)}) async-start(bf16[64,4,256]{2,1,0:T(4,128)(2,1)} %copy.232), calls=%async_computation.1 | async-start | bytes 262144 | tf_op jit(solution)/shard_map/while/body/eval_jaxpr/all_to_all | solution.py:104
  411.6 21.9 %all-to-all-start = ((bf16[64,4,256]{2,1,0:T(4,128)(2,1)}), bf16[64,4,256]{2,1,0:T(4,128)(2,1)S(1)}, u32[]{:S(2)}, u32[]{:S(2)}) async-start(bf16[64,4,256]{2,1,0:T(4,128)(2,1)} %copy.230), calls=%async_computation | async-start | bytes 262144 | tf_op jit(solution)/shard_map/while/body/eval_jaxpr/all_to_all | solution.py:99
  437.4 21.0 %all-to-all-start.1 = ((bf16[64,4,256]{2,1,0:T(4,128)(2,1)}), bf16[64,4,256]{2,1,0:T(4,128)(2,1)S(1)}, u32[]{:S(2)}, u32[]{:S(2)}) async-start(bf16[64,4,256]{2,1,0:T(4,128)(2,1)} %copy.232), calls=%async_computation.1 | async-start | bytes 262144 | tf_op jit(solution)/shard_map/while/body/eval_jaxpr/all_to_all | solution.py:104
  471.1 21.9 %all-to-all-start = ((bf16[64,4,256]{2,1,0:T(4,128)(2,1)}), bf16[64,4,256]{2,1,0:T(4,128)(2,1)S(1)}, u32[]{:S(2)}, u32[]{:S(2)}) async-start(bf16[64,4,256]{2,1,0:T(4,128)(2,1)} %copy.230), calls=%async_computation | async-start | bytes 262144 | tf_op jit(solution)/shard_map/while/body/eval_jaxpr/all_to_all | solution.py:99
  496.9 21.0 %all-to-all-start.1 = ((bf16[64,4,256]{2,1,0:T(4,128)(2,1)}), bf16[64,4,256]{2,1,0:T(4,128)(2,1)S(1)}, u32[]{:S(2)}, u32[]{:S(2)}) async-start(bf16[64,4,256]{2,1,0:T(4,128)(2,1)} %copy.232), calls=%async_computation.1 | async-start | bytes 262144 | tf_op jit(solution)/shard_map/while/body/eval_jaxpr/all_to_all | solution.py:104
  530.7 21.9 %all-to-all-start = ((bf16[64,4,256]{2,1,0:T(4,128)(2,1)}), bf16[64,4,256]{2,1,0:T(4,128)(2,1)S(1)}, u32[]{:S(2)}, u32[]{:S(2)}) async-start(bf16[64,4,256]{2,1,0:T(4,128)(2,1)} %copy.230), calls=%async_computation | async-start | bytes 262144 | tf_op jit(solution)/shard_map/while/body/eval_jaxpr/all_to_all | solution.py:99
  556.5 21.0 %all-to-all-start.1 = ((bf16[64,4,256]{2,1,0:T(4,128)(2,1)}), bf16[64,4,256]{2,1,0:T(4,128)(2,1)S(1)}, u32[]{:S(2)}, u32[]{:S(2)}) async-start(bf16[64,4,256]{2,1,0:T(4,128)(2,1)} %copy.232), calls=%async_computation.1 | async-start | bytes 262144 | tf_op jit(solution)/shard_map/while/body/eval_jaxpr/all_to_all | solution.py:104
  590.2 21.9 %all-to-all-start = ((bf16[64,4,256]{2,1,0:T(4,128)(2,1)}), bf16[64,4,256]{2,1,0:T(4,128)(2,1)S(1)}, u32[]{:S(2)}, u32[]{:S(2)}) async-start(bf16[64,4,256]{2,1,0:T(4,128)(2,1)} %copy.230), calls=%async_computation | async-start | bytes 262144 | tf_op jit(solution)/shard_map/while/body/eval_jaxpr/all_to_all | solution.py:99
  616.0 21.0 %all-to-all-start.1 = ((bf16[64,4,256]{2,1,0:T(4,128)(2,1)}), bf16[64,4,256]{2,1,0:T(4,128)(2,1)S(1)}, u32[]{:S(2)}, u32[]{:S(2)}) async-start(bf16[64,4,256]{2,1,0:T(4,128)(2,1)} %copy.232), calls=%async_computation.1 | async-start | bytes 262144 | tf_op jit(solution)/shard_map/while/body/eval_jaxpr/all_to_all | solution.py:104
  649.8 21.9 %all-to-all-start = ((bf16[64,4,256]{2,1,0:T(4,128)(2,1)}), bf16[64,4,256]{2,1,0:T(4,128)(2,1)S(1)}, u32[]{:S(2)}, u32[]{:S(2)}) async-start(bf16[64,4,256]{2,1,0:T(4,128)(2,1)} %copy.230), calls=%async_computation | async-start | bytes 262144 | tf_op jit(solution)/shard_map/while/body/eval_jaxpr/all_to_all | solution.py:99
  675.6 21.0 %all-to-all-start.1 = ((bf16[64,4,256]{2,1,0:T(4,128)(2,1)}), bf16[64,4,256]{2,1,0:T(4,128)(2,1)S(1)}, u32[]{:S(2)}, u32[]{:S(2)}) async-start(bf16[64,4,256]{2,1,0:T(4,128)(2,1)} %copy.232), calls=%async_computation.1 | async-start | bytes 262144 | tf_op jit(solution)/shard_map/while/body/eval_jaxpr/all_to_all | solution.py:104
  709.3 21.9 %all-to-all-start = ((bf16[64,4,256]{2,1,0:T(4,128)(2,1)}), bf16[64,4,256]{2,1,0:T(4,128)(2,1)S(1)}, u32[]{:S(2)}, u32[]{:S(2)}) async-start(bf16[64,4,256]{2,1,0:T(4,128)(2,1)} %copy.230), calls=%async_computation | async-start | bytes 262144 | tf_op jit(solution)/shard_map/while/body/eval_jaxpr/all_to_all | solution.py:99
  735.2 21.0 %all-to-all-start.1 = ((bf16[64,4,256]{2,1,0:T(4,128)(2,1)}), bf16[64,4,256]{2,1,0:T(4,128)(2,1)S(1)}, u32[]{:S(2)}, u32[]{:S(2)}) async-start(bf16[64,4,256]{2,1,0:T(4,128)(2,1)} %copy.232), calls=%async_computation.1 | async-start | bytes 262144 | tf_op jit(solution)/shard_map/while/body/eval_jaxpr/all_to_all | solution.py:104
  768.9 21.9 %all-to-all-start = ((bf16[64,4,256]{2,1,0:T(4,128)(2,1)}), bf16[64,4,256]{2,1,0:T(4,128)(2,1)S(1)}, u32[]{:S(2)}, u32[]{:S(2)}) async-start(bf16[64,4,256]{2,1,0:T(4,128)(2,1)} %copy.230), calls=%async_computation | async-start | bytes 262144 | tf_op jit(solution)/shard_map/while/body/eval_jaxpr/all_to_all | solution.py:99
  794.7 21.0 %all-to-all-start.1 = ((bf16[64,4,256]{2,1,0:T(4,128)(2,1)}), bf16[64,4,256]{2,1,0:T(4,128)(2,1)S(1)}, u32[]{:S(2)}, u32[]{:S(2)}) async-start(bf16[64,4,256]{2,1,0:T(4,128)(2,1)} %copy.232), calls=%async_computation.1 | async-start | bytes 262144 | tf_op jit(solution)/shard_map/while/body/eval_jaxpr/all_to_all | solution.py:104
  828.4 21.9 %all-to-all-start = ((bf16[64,4,256]{2,1,0:T(4,128)(2,1)}), bf16[64,4,256]{2,1,0:T(4,128)(2,1)S(1)}, u32[]{:S(2)}, u32[]{:S(2)}) async-start(bf16[64,4,256]{2,1,0:T(4,128)(2,1)} %copy.230), calls=%async_computation | async-start | bytes 262144 | tf_op jit(solution)/shard_map/while/body/eval_jaxpr/all_to_all | solution.py:99
  888.0 21.9 %all-to-all-start = ((bf16[64,4,256]{2,1,0:T(4,128)(2,1)}), bf16[64,4,256]{2,1,0:T(4,128)(2,1)S(1)}, u32[]{:S(2)}, u32[]{:S(2)}) async-start(bf16[64,4,256]{2,1,0:T(4,128)(2,1)} %copy.230), calls=%async_computation | async-start | bytes 262144 | tf_op jit(solution)/shard_map/while/body/eval_jaxpr/all_to_all | solution.py:99
  947.0 22.0 %all-to-all-start.4 = ((bf16[64,4,256]{2,1,0:T(4,128)(2,1)}), bf16[64,4,256]{2,1,0:T(4,128)(2,1)S(1)}, u32[]{:S(2)}, u32[]{:S(2)}) async-start(bf16[64,4,256]{2,1,0:T(4,128)(2,1)} %copy.146), calls=%async_computation.4 | async-start | bytes 262144 | tf_op jit(solution)/shard_map/all_to_all | solution.py:99
  972.4 21.2 %all-to-all-start.5 = ((bf16[64,4,256]{2,1,0:T(4,128)(2,1)}), bf16[64,4,256]{2,1,0:T(4,128)(2,1)S(1)}, u32[]{:S(2)}, u32[]{:S(2)}) async-start(bf16[64,4,256]{2,1,0:T(4,128)(2,1)} %copy.151), calls=%async_computation.5 | async-start | bytes 262144 | tf_op jit(solution)/shard_map/all_to_all | solution.py:104
  (183 other events, 1329.5 us)
where the time goes:
time: 1010 us; the launch traced here: 998 us
  waiting for transfers between devices  583 us (58%)
  starting transfers between devices  211 us (21%)
  matrix products  115 us (11%)
  local copies, waits for them, and re-layouts  67.5 us (7%)
  other arithmetic  17.3 us (2%)
    all_to_all x16, waiting for transfers between devices, one_step(): lax.all_to_all(lower_gradient, 'tensor', split_axis=0, concat_axis=1, til...  252 us
    all_to_all x16, waiting for transfers between devices, one_step(): lax.all_to_all(grad_up, 'tensor', split_axis=0, concat_axis=1, tiled=True)  236 us
    dot_general x131, matrix products, matrix_product(): jnp.einsum(form, left_side, right_side, preferred_element_type=jnp.float32)  115 us
    all_to_all x16, starting transfers between devices, one_step(): lax.all_to_all(lower_gradient, 'tensor', split_axis=0, concat_axis=1, til...  91.7 us
    all_to_all x16, starting transfers between devices, one_step(): lax.all_to_all(grad_up, 'tensor', split_axis=0, concat_axis=1, tiled=True)  77.7 us
    ppermute x15, waiting for transfers between devices, passed_along(): lax.ppermute(value, axis, [(source, source + steps) for source in range(l...  66.3 us
    while x300, local copies, waits for them, and re-layouts  21.7 us
  transfers between devices with their start and end apart: 49, of which 49 were waited for; matrix products, arithmetic and copies ran while one was open for 6% of the time, Pallas kernels for 0%

commit v1 on v0

v1 whole, which is shorter than its diff:
```python
import jax
import jax.numpy as jnp
from jax import lax
from jax.experimental import pallas as pl
from jax.experimental.pallas import tpu as pltpu
from jax.sharding import PartitionSpec as P

SQRT_TWO_PI = 0.7978845608028654
CUBIC_TERM = 0.044715
MIB = 2**20

IN_VMEM = pl.BlockSpec(memory_space=pltpu.VMEM)
IN_SMEM = pl.BlockSpec(memory_space=pltpu.SMEM)
IN_PLACE = pl.BlockSpec(memory_space=pl.ANY)


def gelu_tanh(linear):
    inner = SQRT_TWO_PI * (linear + CUBIC_TERM * linear * linear * linear)
    return 0.5 * linear * (1.0 + jnp.tanh(inner))


def gelu_slope(linear):
    inner = SQRT_TWO_PI * (linear + CUBIC_TERM * linear * linear * linear)
    tangent = jnp.tanh(inner)
    return 0.5 * (1.0 + tangent) + 0.5 * linear * (1.0 - tangent * tangent) * SQRT_TWO_PI * (
        1.0 + 3.0 * CUBIC_TERM * linear * linear
    )


def matrix_product(form, left_side, right_side):
    return jnp.einsum(form, left_side, right_side, preferred_element_type=jnp.float32)


def exchange_blocks(source, target, blocks, rows):
    for row in range(rows):
        turned = source[pl.ds(row, blocks, stride=rows), :].T
        target[pl.ds(row, blocks, stride=rows), :] = jnp.concatenate(
            [turned[:blocks], turned[blocks:]], axis=1
        )


def load_second_body(gathered, second, sems):
    copy = pltpu.make_async_copy(gathered, second, sems.at[0])
    copy.start()
    copy.wait()


def load_rest_body(gathered, fourth, third, first, sems):
    hidden = third.shape[3]
    width = third.shape[2]
    copies = []
    for half in range(2):
        copies.append((gathered.at[:, pl.ds(half * width, width), :], fourth.at[:, half]))
    base = 2 * width
    for half in range(2):
        for part in range(hidden // width):
            start = base + half * hidden + part * width
            copies.append(
                (
                    gathered.at[:, pl.ds(start, width), :],
                    third.at[:, half, :, pl.ds(part * width, width)],
                )
            )
    base = base + 2 * hidden
    for half in range(2):
        copies.append((gathered.at[:, pl.ds(base + half * width, width), :], first.at[:, half]))
    started = [
        pltpu.make_async_copy(source, target, sems.at[number])
        for number, (source, target) in enumerate(copies)
    ]
    for copy in started:
        copy.start()
    for copy in started:
        copy.wait()


def slope_body(raised, second, slope, rows_in, rows_out):
    blocks, rows, width = raised.shape
    rows_in[...] = raised[...].astype(jnp.float32).reshape(blocks * rows, width)
    exchange_blocks(rows_in, rows_out, blocks, rows)
    for b in range(blocks):
        mixed = rows_out[pl.ds(b * rows, rows), :].astype(jnp.bfloat16)
        linear = lax.dot_general(
            mixed,
            second[b // 2, b % 2],
            (((1,), (1,)), ((), ())),
            preferred_element_type=jnp.float32,
        )
        slope[b] = gelu_slope(linear)


def section_body(
    active,
    cotangent,
    old_cotangent,
    old_gv,
    old_gu,
    slope,
    fourth,
    third,
    second,
    first,
    result,
    kept_cotangent,
    kept_gv,
    kept_gu,
    rows_in,
    rows_out,
    grad_lin,
):
    blocks, rows, width = cotangent.shape

    @pl.when(active[0] == 0)
    def _():
        result[...] = cotangent[...]
        kept_cotangent[...] = old_cotangent[...]
        kept_gv[...] = old_gv[...]
        kept_gu[...] = old_gu[...]

    @pl.when(active[0] != 0)
    def _():
        kept_cotangent[...] = cotangent[...]
        for a in range(blocks):
            rows_in[pl.ds(a * rows, rows), :] = jnp.dot(
                cotangent[a], fourth[a // 2, a % 2], preferred_element_type=jnp.float32
            )
        exchange_blocks(rows_in, rows_out, blocks, rows)
        kept_gv[...] = rows_out[...].reshape(blocks, rows, width).astype(jnp.bfloat16)
        for b in range(blocks):
            grad_hid = jnp.dot(
                kept_gv[b], third[b // 2, b % 2], preferred_element_type=jnp.float32
            )
            grad_lin[b] = (grad_hid * slope[b]).astype(jnp.bfloat16)
        for b in range(blocks):
            rows_in[pl.ds(b * rows, rows), :] = jnp.dot(
                grad_lin[b], second[b // 2, b % 2], preferred_element_type=jnp.float32
            )
        exchange_blocks(rows_in, rows_out, blocks, rows)
        kept_gu[...] = rows_out[...].reshape(blocks, rows, width).astype(jnp.bfloat16)
        for a in range(blocks):
            term = jnp.dot(kept_gu[a], first[a // 2, a % 2], preferred_element_type=jnp.float32)
            result[a] = (cotangent[a].astype(jnp.float32) + term).astype(jnp.bfloat16)


def load_second(gathered, devices, hidden, width):
    return pl.pallas_call(
        load_second_body,
        out_shape=pltpu.VMEM((devices, 2, hidden, width), jnp.bfloat16),
        in_specs=[IN_PLACE],
        out_specs=IN_VMEM,
        scratch_shapes=[pltpu.SemaphoreType.DMA((1,))],
        compiler_params=pltpu.CompilerParams(vmem_limit_bytes=16 * MIB),
        name="load_second",
    )(gathered)


def load_rest(gathered, devices, hidden, width):
    return pl.pallas_call(
        load_rest_body,
        out_shape=[
            pltpu.VMEM((devices, 2, width, width), jnp.bfloat16),
            pltpu.VMEM((devices, 2, width, hidden), jnp.bfloat16),
            pltpu.VMEM((devices, 2, width, width), jnp.bfloat16),
        ],
        in_specs=[IN_PLACE],
        out_specs=[IN_VMEM] * 3,
        scratch_shapes=[pltpu.SemaphoreType.DMA((4 + 2 * (hidden // width),))],
        compiler_params=pltpu.CompilerParams(vmem_limit_bytes=24 * MIB),
        name="load_rest",
    )(gathered)


def row_slopes(raised, second):
    blocks, rows, width = raised.shape
    hidden = second.shape[2]
    return pl.pallas_call(
        slope_body,
        out_shape=jax.ShapeDtypeStruct((blocks, rows, hidden), jnp.float32),
        in_specs=[IN_VMEM] * 2,
        out_specs=IN_VMEM,
        scratch_shapes=[pltpu.VMEM((blocks * rows, width), jnp.float32)] * 2,
        compiler_params=pltpu.CompilerParams(vmem_limit_bytes=12 * MIB),
        name="row_slopes",
    )(raised, second)


def section_step(active, cotangent, kept, slope, weights):
    blocks, rows, width = cotangent.shape
    hidden = slope.shape[2]
    return pl.pallas_call(
        section_body,
        out_shape=[jax.ShapeDtypeStruct(cotangent.shape, jnp.bfloat16)] * 4,
        in_specs=[IN_SMEM] + [IN_VMEM] * 9,
        out_specs=[IN_VMEM] * 4,
        scratch_shapes=[pltpu.VMEM((blocks * rows, width), jnp.float32)] * 2
        + [pltpu.VMEM((blocks, rows, hidden), jnp.bfloat16)],
        compiler_params=pltpu.CompilerParams(vmem_limit_bytes=12 * MIB),
        name="section_step",
    )(active, cotangent, *kept, slope, *weights)


def to_owners(value):
    return lax.all_to_all(value, "tensor", split_axis=0, concat_axis=0, tiled=True)


def local(section_inputs, out_grad, w1, w2, w3, w4):
    devices = lax.axis_size("tensor")
    section_count = lax.axis_size("section")
    section_id = lax.axis_index("section")
    all_rows = section_inputs.shape[1] * section_inputs.shape[2]
    owned = w1.shape[1]
    width = w1.shape[2]
    hidden = w2.shape[3]
    blocks = owned * devices
    spread = width // blocks
    rows = all_rows // devices
    parts = hidden // width

    natural = lax.broadcasted_iota(jnp.int32, (width, width), 0)
    grouped = lax.broadcasted_iota(jnp.int32, (width, width), 1)
    reorder = (grouped == (natural % spread) * blocks + natural // spread).astype(jnp.bfloat16)

    second_local = matrix_product("bkn,kp->bnp", w2[0], reorder).astype(jnp.bfloat16)
    fourth_local = matrix_product("akc,kp->acp", w4[0], reorder).astype(jnp.bfloat16)
    third_local = matrix_product(
        "bqnk,kp->bqpn", w3[0].reshape(owned, parts, width, width), reorder
    ).astype(jnp.bfloat16)
    first_local = matrix_product("ack,kp->apc", w1[0], reorder).astype(jnp.bfloat16)
    rest_local = jnp.concatenate(
        [
            fourth_local.reshape(owned * width, width),
            third_local.reshape(owned * hidden, width),
            first_local.reshape(owned * width, width),
        ],
        axis=0,
    )
    second_all = lax.all_gather(second_local, "tensor", axis=0, tiled=False)
    rest_all = lax.all_gather(rest_local, "tensor", axis=0, tiled=False)

    input_rows = section_inputs[0].reshape(all_rows, owned, width)
    raised_rows = matrix_product("owz,wzy->wyo", input_rows, w1[0]).astype(jnp.bfloat16)
    raised_grouped = matrix_product("tac,apc->atp", input_rows, first_local).astype(jnp.bfloat16)
    raised_grouped = raised_grouped.reshape(owned, devices, rows, width).transpose(1, 0, 2, 3)
    targets = out_grad.reshape(devices, rows, owned, width).transpose(0, 2, 1, 3)
    by_rows = to_owners(jnp.concatenate([raised_grouped, targets], axis=2))
    by_rows = by_rows.reshape(blocks, 2 * rows, width)
    raised_here = by_rows[:, :rows]
    cotangent = by_rows[:, rows:]

    mixed = lax.all_to_all(raised_rows, "tensor", split_axis=1, concat_axis=0, tiled=True)
    mixed = mixed.reshape(blocks, owned, spread, all_rows)
    linear = matrix_product("abrt,barn->btn", mixed, w2[0].reshape(owned, blocks, spread, hidden))
    gelu_out = gelu_tanh(linear).astype(jnp.bfloat16)
    slope_owned = gelu_slope(linear)
    lowered = matrix_product("btn,bnk->bkt", gelu_out, w3[0]).astype(jnp.bfloat16)
    handed_back = lax.all_to_all(lowered, "tensor", split_axis=1, concat_axis=0, tiled=True)
    handed_back = handed_back.reshape(blocks, owned, spread, all_rows)

    second = load_second(second_all, devices, hidden, width)
    slope = row_slopes(raised_here, second)
    fourth, third, first = load_rest(rest_all, devices, hidden, width)
    weights = (fourth, third, second, first)
    kept = (cotangent, cotangent, cotangent)
    for step in range(section_count):
        turn = section_count - 1 - step
        active = (section_id == turn).astype(jnp.int32).reshape(1)
        cotangent, *kept = section_step(active, cotangent, kept, slope, weights)
        if turn > 0:
            cotangent = lax.ppermute(cotangent, "section", [(turn, turn - 1)])

    sent = jnp.concatenate(kept, axis=1).reshape(devices, owned, 3, rows, width)
    returned = to_owners(sent)
    returned = returned.transpose(2, 1, 0, 3, 4).reshape(3, owned, all_rows, width)
    gy, gv, gu = returned[0], returned[1], returned[2]
    grad_inputs = gy.astype(jnp.float32) + matrix_product("atp,apc->atc", gu, first_local)
    grad_inputs = grad_inputs.astype(jnp.bfloat16).transpose(1, 0, 2)
    grad_hid = matrix_product("btp,bqpn->btqn", gv, third_local).reshape(owned, all_rows, hidden)
    grad_lin = (grad_hid * slope_owned).astype(jnp.bfloat16)
    gv = matrix_product("btp,kp->btk", gv, reorder).astype(jnp.bfloat16)
    gu = matrix_product("atp,kp->atk", gu, reorder).astype(jnp.bfloat16)
    grad_w1 = matrix_product("tac,atk->ack", input_rows, gu)
    grad_w2 = matrix_product("abrt,btn->barn", mixed, grad_lin).reshape(owned, width, hidden)
    grad_w3 = matrix_product("btn,btk->bnk", gelu_out, gv)
    grad_w4 = matrix_product("nxpq,xqf->xnpf", handed_back, gy).reshape(owned, width, width)
    grad_inputs = grad_inputs.reshape(section_inputs.shape)
    return (grad_inputs, grad_w1[None], grad_w2[None], grad_w3[None], grad_w4[None])


def solution(mesh):
    in_specs = (
        P("section", None, None, "tensor"),
        P(None, None, "tensor"),
        P("section", "tensor", None, None),
        P("section", "tensor", None, None),
        P("section", "tensor", None, None),
        P("section", "tensor", None, None),
    )
    out_specs = (
        P("section", None, None, "tensor"),
        P("section", "tensor", None, None),
        P("section", "tensor", None, None),
        P("section", "tensor", None, None),
        P("section", "tensor", None, None),
    )
    return jax.shard_map(local, mesh=mesh, in_specs=in_specs, out_specs=out_specs, check_vma=False)
```

time: 1010 us -> 630 us (0.62)
  waiting for transfers between devices: 583 us -> 268 us
  local copies, waits for them, and re-layouts: 67.5 us -> 225 us
  starting transfers between devices: 211 us -> 72 us
  matrix products: 115 us -> 11 us
  Pallas kernels: 0 us -> 27.3 us
  other arithmetic: 17.3 us -> 1.72 us
  between operations: 1.03 us -> 15.3 us
    all_to_all x32 -> x2, waiting for transfers between devices: 488 us -> 50.5 us  [to_owners(): lax.all_to_all(value, 'tensor', split_axis=0, concat_axis=0, tiled=True)]
    unnamed x38 -> x298, local copies, waits for them, and re-layouts: 5.32 us -> 208 us
    all_to_all x32 -> x2, starting transfers between devices: 169 us -> 37.5 us  [to_owners(): lax.all_to_all(value, 'tensor', split_axis=0, concat_axis=0, tiled=True)]
    all_gather x0 -> x2, waiting for transfers between devices: none -> 123 us  [the longest x1 75.2 us: local(): rest_all = lax.all_gather(rest_local, 'tensor', axis=0, tiled=False)]
    dot_general x131 -> x12, matrix products: 115 us -> 10.7 us  [matrix_product(): jnp.einsum(form, left_side, right_side, preferred_element_type=jnp.float32)]
    ppermute x15, waiting for transfers between devices: 66.3 us -> 93.7 us  [local(): cotangent = lax.ppermute(cotangent, 'section', [(turn, turn - 1)])]
    pallas_call x0 -> x19, Pallas kernels: none -> 27.3 us  [the longest x16 22.2 us: section_step(): pl.pallas_call(section_body, out_shape=[jax.ShapeDtypeStruct(cotangent.sh...]
    while x301 -> x0, local copies, waits for them, and re-layouts: 21.9 us -> none
  transfers between devices with their start and end apart: 49 -> 21, of which waited for: 49 -> 5; matrix products, arithmetic and copies ran while one was open for 6% -> 3% of each run, Pallas kernels for 0% -> 2%
where the time goes in v1:
time: 630 us; the launch traced here: 620 us
  waiting for transfers between devices  268 us (43%)
  local copies, waits for them, and re-layouts  225 us (36%)
  starting transfers between devices  72 us (11%)
  Pallas kernels  27.3 us (4%)
  between operations  15.3 us (2%)
  matrix products  11 us (2%)
    unnamed x298, local copies, waits for them, and re-layouts  208 us
    ppermute x15, waiting for transfers between devices, local(): cotangent = lax.ppermute(cotangent, 'section', [(turn, turn - 1)])  93.7 us
    all_gather x1, waiting for transfers between devices, local(): rest_all = lax.all_gather(rest_local, 'tensor', axis=0, tiled=False)  75.2 us
    all_to_all x2, waiting for transfers between devices, to_owners(): lax.all_to_all(value, 'tensor', split_axis=0, concat_axis=0, tiled=True)  50.5 us
    all_gather x1, waiting for transfers between devices, local(): second_all = lax.all_gather(second_local, 'tensor', axis=0, tiled=False)  48.3 us
    all_to_all x2, starting transfers between devices, to_owners(): lax.all_to_all(value, 'tensor', split_axis=0, concat_axis=0, tiled=True)  37.5 us
    pallas_call x16, Pallas kernels, section_step(): pl.pallas_call(section_body, out_shape=[jax.ShapeDtypeStruct(cotangent.sh...  22.2 us
    ppermute x15, starting transfers between devices, local(): cotangent = lax.ppermute(cotangent, 'section', [(turn, turn - 1)])  14.4 us
  transfers between devices with their start and end apart: 21, of which 5 were waited for; matrix products, arithmetic and copies ran while one was open for 3% of the time, Pallas kernels for 2%

profile of v1, /device:TPU:1, one launch (start us, length us, event | category | flops | bytes accessed | tf_op | source)
XLA Modules:
  0.0 619.6 jit_solution(7691248231730819576)
XLA Ops:
  16.3 16.7 %all-to-all-start = ((bf16[32,2,16,128]{3,2,1,0:T(8,128)(2,1)}), bf16[32,2,16,128]{3,2,1,0:T(8,128)(2,1)S(1)}, u32[]{:S(2)}, u32[]{:S(2)}) async-start(bf16[32,2,16,128]{3,2,1,0:T(8,128)(2,1)} %copy.85), calls=%async_computation | async-start | bytes 524288 | tf_op jit(solution)/shard_map/all_to_all | solution.py:203
  33.1 24.9 %all-to-all-done = bf16[32,2,16,128]{3,2,1,0:T(8,128)(2,1)S(1)} async-done(((bf16[32,2,16,128]{3,2,1,0:T(8,128)(2,1)}), bf16[32,2,16,128]{3,2,1,0:T(8,128)(2,1)S(1)}, u32[]{:S(2)}, u32[]{:S(2)}) %all-to-all-start) | async-done | bytes 262176 | tf_op jit(solution)/shard_map/all_to_all | solution.py:203
  58.0 48.3 %all-gather.5.cloned.1.call-done = bf16[64,512,128]{2,1,0:T(8,128)(2,1)} async-done(((bf16[2,512,128]{2,1,0:T(8,128)(2,1)}), bf16[64,512,128]{2,1,0:T(8,128)(2,1)}) %all-gather.5.cloned.1.call-update) | async-done | bytes 8388624 | tf_op jit(solution)/shard_map/all_gather | solution.py:237
  116.1 75.2 %all-gather.7.cloned.1.call-done = bf16[49152,128]{1,0:T(8,128)(2,1)} async-done(((bf16[1536,128]{1,0:T(8,128)(2,1)}), bf16[49152,128]{1,0:T(8,128)(2,1)}) %all-gather.7.cloned.1.call-update) | async-done | bytes 12582928 | tf_op jit(solution)/shard_map/all_gather | solution.py:238
  191.3 4.7 copy-done.50
  202.8 3.4 copy-done.19
  215.2 3.4 copy-done.20
  227.4 3.4 copy-done.4
  230.8 3.4 copy-done.21
  245.9 3.4 copy-done.22
  257.9 3.4 copy-done.6
  261.3 3.4 copy-done.23
  276.8 3.4 copy-done.24
  288.8 3.4 copy-done.8
  292.1 3.4 copy-done.25
  307.3 3.4 copy-done.26
  320.4 7.9 %all-to-all-start.2 = ((bf16[2,128,256]{2,0,1:T(2,128)(2,1)}), bf16[2,128,256]{2,0,1:T(2,128)(2,1)}, u32[]{:S(2)}, u32[]{:S(2)}) async-start(bf16[2,128,256]{2,0,1:T(2,128)(2,1)} %copy.97), calls=%async_computation.2 | async-start | bytes 262144 | tf_op jit(solution)/shard_map/all_to_all | solution.py:250
  331.7 3.4 copy-done.27
  346.2 3.4 copy-done.28
  361.3 3.4 copy-done.29
  378.5 3.4 copy-done.13
  381.8 3.4 copy-done.30
  390.8 3.8 copy-done.14
  400.6 12.2 %all-to-all-start.3 = ((bf16[2,128,256]{2,0,1:T(2,128)(2,1)}), bf16[2,128,256]{2,0,1:T(2,128)(2,1)}, u32[]{:S(2)}, u32[]{:S(2)}) async-start(bf16[2,128,256]{2,0,1:T(2,128)(2,1)} %copy.105), calls=%async_computation.3 | async-start | bytes 262144 | tf_op jit(solution)/shard_map/all_to_all | solution.py:256
  416.3 3.4 copy-done.31
  431.7 3.4 copy-done.32
  443.6 93.7 %collective-permute-done.14.cotangent = bf16[64,8,128]{2,1,0:T(8,128)(2,1)} collective-permute-done((bf16[64,8,128]{2,1,0:T(8,128)(2,1)}, bf16[64,8,128]{2,1,0:T(8,128)(2,1)}, u32[]{:S(2)}, u32[]{:S(2)}) %collective-permute-start.14) | collective-permute-done | bytes 131104 | tf_op jit(solution)/shard_map/ppermute | solution.py:269
  537.3 3.4 copy-done.17
  540.7 3.4 copy-done.33
  547.5 5.7 section_step.31
  554.1 20.7 %all-to-all-start.1 = ((bf16[32,2,3,8,128]{4,3,2,1,0:T(8,128)(2,1)}), bf16[32,2,3,8,128]{4,3,2,1,0:T(8,128)(2,1)S(1)}, u32[]{:S(2)}, u32[]{:S(2)}) async-start(bf16[32,2,3,8,128]{4,3,2,1,0:T(8,128)(2,1)} %bitcast.41), calls=%async_computation.1 | async-start | bytes 786432 | tf_op jit(solution)/shard_map/all_to_all | solution.py:203
  577.0 25.7 %all-to-all-done.1 = bf16[32,2,3,8,128]{4,3,2,1,0:T(8,128)(2,1)S(1)} async-done(((bf16[32,2,3,8,128]{4,3,2,1,0:T(8,128)(2,1)}), bf16[32,2,3,8,128]{4,3,2,1,0:T(8,128)(2,1)S(1)}, u32[]{:S(2)}, u32[]{:S(2)}) %all-to-all-start.1) | async-done | bytes 393248 | tf_op jit(solution)/shard_map/all_to_all | solution.py:203
  (369 shorter events, 196.4 us)
Async XLA Ops:
  7.2 4.9 copy-start
  7.2 99.1 %all-gather.5.cloned.1.call-start = ((), (), s32[]{:S(2)}) async-start(), calls=%async_computation.4 | async-start | bytes 8650752 | tf_op jit(solution)/shard_map/all_gather | solution.py:237
  7.3 6.0 copy-start.144
  7.3 6.0 copy-start.146
  9.5 181.8 %all-gather.7.cloned.1.call-start = ((), (), s32[]{:S(2)}) async-start(), calls=%async_computation.5 | async-start | bytes 12976128 | tf_op jit(solution)/shard_map/all_gather | solution.py:238
  12.5 97.8 %copy-start.134 = (bf16[128,2,4,128]{3,0,2,1:T(8,128)(2,1)}, bf16[128,2,4,128]{3,0,2,1:T(8,128)(2,1)S(1)}, u32[]{:S(2)}) copy-start(bf16[128,2,4,128]{3,0,2,1:T(8,128)(2,1)S(1)} %convolution_convert_fusion) | copy-start | bytes 786436
  14.3 96.0 %copy-start.135 = (bf16[256,2,128]{2,1,0:T(2,128)(2,1)}, bf16[256,2,128]{2,1,0:T(2,128)(2,1)S(1)}, u32[]{:S(2)}) copy-start(bf16[256,2,128]{2,1,0:T(2,128)(2,1)S(1)} %reshape_squeeze.9) | copy-start | bytes 393220
  16.3 41.6 %all-to-all-start = ((bf16[32,2,16,128]{3,2,1,0:T(8,128)(2,1)}), bf16[32,2,16,128]{3,2,1,0:T(8,128)(2,1)S(1)}, u32[]{:S(2)}, u32[]{:S(2)}) async-start(bf16[32,2,16,128]{3,2,1,0:T(8,128)(2,1)} %copy.85), calls=%async_computation | async-start | bytes 524288 | tf_op jit(solution)/shard_map/all_to_all | solution.py:203
  191.3 11.6 %copy-start.2 = (bf16[32,2,512,128]{3,2,1,0:T(8,128)(2,1)S(1)}, bf16[32,2,512,128]{3,2,1,0:T(8,128)(2,1)}, u32[]{:S(2)}) copy-start(bf16[32,2,512,128]{3,2,1,0:T(8,128)(2,1)} %copy-done.1) | copy-start | bytes 25165828
  210.5 0.7 collective-permute-start
  226.1 1.3 collective-permute-start.1
  241.2 0.7 collective-permute-start.2
  256.6 1.3 collective-permute-start.3
  272.1 0.7 collective-permute-start.4
  287.5 1.3 collective-permute-start.5
  302.5 0.7 collective-permute-start.6
  318.1 10.2 %collective-permute-start.7 = (bf16[64,8,128]{2,1,0:T(8,128)(2,1)}, bf16[64,8,128]{2,1,0:T(8,128)(2,1)}, u32[]{:S(2)}, u32[]{:S(2)}) collective-permute-start(bf16[64,8,128]{2,1,0:T(8,128)(2,1)} %get-tuple-element.102), channel_id=1, source_target_pairs={{256,224},{257,225},{258,226},{259,227},{260,228},{261,229},{262,2... | collective-permute-start | bytes 393224 | tf_op jit(solution)/shard_map/ppermute | solution.py:269
  320.4 54.8 %all-to-all-start.2 = ((bf16[2,128,256]{2,0,1:T(2,128)(2,1)}), bf16[2,128,256]{2,0,1:T(2,128)(2,1)}, u32[]{:S(2)}, u32[]{:S(2)}) async-start(bf16[2,128,256]{2,0,1:T(2,128)(2,1)} %copy.97), calls=%async_computation.2 | async-start | bytes 262144 | tf_op jit(solution)/shard_map/all_to_all | solution.py:250
  342.1 0.7 collective-permute-start.8
  356.6 0.7 collective-permute-start.9
  372.1 6.3 %collective-permute-start.10 = (bf16[64,8,128]{2,1,0:T(8,128)(2,1)}, bf16[64,8,128]{2,1,0:T(8,128)(2,1)}, u32[]{:S(2)}, u32[]{:S(2)}) collective-permute-start(bf16[64,8,128]{2,1,0:T(8,128)(2,1)} %get-tuple-element.114), channel_id=1, source_target_pairs={{160,128},{161,129},{162,130},{163,131},{164,132},{165,133},{166,1... | collective-permute-start | bytes 393224 | tf_op jit(solution)/shard_map/ppermute | solution.py:269
  389.7 1.1 collective-permute-start.11
  390.7 7.1 %copy-start.138 = (f32[2,256,512]{2,1,0:T(8,128)}, f32[2,256,512]{2,1,0:T(8,128)S(1)}, u32[]{:S(2)}) copy-start(f32[2,256,512]{2,1,0:T(8,128)S(1)} %convolution_bitcast_fusion) | copy-start | bytes 3145732
  396.5 16.4 %collective-permute-start.12 = (bf16[64,8,128]{2,1,0:T(8,128)(2,1)}, bf16[64,8,128]{2,1,0:T(8,128)(2,1)}, u32[]{:S(2)}, u32[]{:S(2)}) collective-permute-start(bf16[64,8,128]{2,1,0:T(8,128)(2,1)} %get-tuple-element.122), channel_id=1, source_target_pairs={{96,64},{97,65},{98,66},{99,67},{100,68},{101,69},{102,70},{103,71... | collective-permute-start | bytes 393224 | tf_op jit(solution)/shard_map/ppermute | solution.py:269
  400.6 153.4 %all-to-all-start.3 = ((bf16[2,128,256]{2,0,1:T(2,128)(2,1)}), bf16[2,128,256]{2,0,1:T(2,128)(2,1)}, u32[]{:S(2)}, u32[]{:S(2)}) async-start(bf16[2,128,256]{2,0,1:T(2,128)(2,1)} %copy.105), calls=%async_computation.3 | async-start | bytes 262144 | tf_op jit(solution)/shard_map/all_to_all | solution.py:256
  426.9 0.7 collective-permute-start.13
  442.3 95.0 %collective-permute-start.14 = (bf16[64,8,128]{2,1,0:T(8,128)(2,1)}, bf16[64,8,128]{2,1,0:T(8,128)(2,1)}, u32[]{:S(2)}, u32[]{:S(2)}) collective-permute-start(bf16[64,8,128]{2,1,0:T(8,128)(2,1)} %get-tuple-element.130), channel_id=1, source_target_pairs={{32,0},{33,1},{34,2},{35,3},{36,4},{37,5},{38,6},{39,7},{40,8},{41... | collective-permute-start | bytes 393224 | tf_op jit(solution)/shard_map/ppermute | solution.py:269
  553.2 55.7 %copy-start.137 = (bf16[256,2,128]{2,1,0:T(2,128)(2,1)S(1)}, bf16[256,2,128]{2,1,0:T(2,128)(2,1)}, u32[]{:S(2)}) copy-start(bf16[256,2,128]{2,1,0:T(2,128)(2,1)} %copy-done.135) | copy-start | bytes 393220
  553.2 55.7 %copy-start.145 = (s32[128]{0:T(128)S(1)}, s32[128]{0:T(128)}, u32[]{:S(2)}) copy-start(s32[128]{0:T(128)} %copy-done.144) | copy-start | bytes 1540
  553.2 55.7 %copy-start.147 = (s32[128]{0:T(128)S(1)}, s32[128]{0:T(128)}, u32[]{:S(2)}) copy-start(s32[128]{0:T(128)} %copy-done.146) | copy-start | bytes 1540
  553.2 56.3 %copy-start.141 = (bf16[128,2,128]{2,0,1:T(8,128)(2,1)S(1)}, bf16[128,2,128]{2,0,1:T(8,128)(2,1)}, u32[]{:S(2)}) copy-start(bf16[128,2,128]{2,0,1:T(8,128)(2,1)} %copy-done.140) | copy-start | bytes 196612
  554.1 48.6 %all-to-all-start.1 = ((bf16[32,2,3,8,128]{4,3,2,1,0:T(8,128)(2,1)}), bf16[32,2,3,8,128]{4,3,2,1,0:T(8,128)(2,1)S(1)}, u32[]{:S(2)}, u32[]{:S(2)}) async-start(bf16[32,2,3,8,128]{4,3,2,1,0:T(8,128)(2,1)} %bitcast.41), calls=%async_computation.1 | async-start | bytes 786432 | tf_op jit(solution)/shard_map/all_to_all | solution.py:203
  (137 other events, 220.5 us)
Sparse Core Ops, SparseCore 0:
  10.1 96.1 all-gather.4
  109.0 82.2 all-gather.6

commit v2 on v0

v2 whole, which is shorter than its diff:
```python
import functools

import jax
import jax.numpy as jnp
from jax import lax
from jax.experimental import pallas as pl
from jax.experimental.pallas import tpu as pltpu
from jax.sharding import PartitionSpec as P

SQRT_TWO_PI = 0.7978845608028654
CUBIC_TERM = 0.044715
MIB = 2**20

IN_VMEM = pl.BlockSpec(memory_space=pltpu.VMEM)
IN_SMEM = pl.BlockSpec(memory_space=pltpu.SMEM)
IN_PLACE = pl.BlockSpec(memory_space=pl.ANY)


def gelu_tanh(linear):
    inner = SQRT_TWO_PI * (linear + CUBIC_TERM * linear * linear * linear)
    return 0.5 * linear * (1.0 + jnp.tanh(inner))


def gelu_slope(linear):
    inner = SQRT_TWO_PI * (linear + CUBIC_TERM * linear * linear * linear)
    tangent = jnp.tanh(inner)
    return 0.5 * (1.0 + tangent) + 0.5 * linear * (1.0 - tangent * tangent) * SQRT_TWO_PI * (
        1.0 + 3.0 * CUBIC_TERM * linear * linear
    )


def matrix_product(form, left_side, right_side):
    return jnp.einsum(form, left_side, right_side, preferred_element_type=jnp.float32)


def exchange_blocks(source, target, blocks, rows):
    for row in range(rows):
        turned = source[pl.ds(row, blocks, stride=rows), :].T
        target[pl.ds(row, blocks, stride=rows), :] = jnp.concatenate(
            [turned[:blocks], turned[blocks:]], axis=1
        )


def contract_last(left_side, right_side):
    return lax.dot_general(
        left_side, right_side, (((1,), (1,)), ((), ())), preferred_element_type=jnp.float32
    )


def order_matrix(width, blocks, spread):
    grouped = lax.broadcasted_iota(jnp.int32, (width, width), 0)
    natural = lax.broadcasted_iota(jnp.int32, (width, width), 1)
    here = grouped == (natural % spread) * blocks + natural // spread
    return jnp.where(here, 1.0, 0.0).astype(jnp.bfloat16)


def prepare_body(blocks, w1, w2, w3, w4, packed):
    owned, width, hidden = w2.shape
    order = order_matrix(width, blocks, width // blocks)
    base = 0
    for b in range(owned):
        turned = jnp.dot(order, w2[b], preferred_element_type=jnp.float32).T
        packed[pl.ds(base, hidden), :] = turned.astype(jnp.bfloat16)
        base += hidden
    for a in range(owned):
        turned = jnp.dot(order, w4[a], preferred_element_type=jnp.float32).T
        packed[pl.ds(base, width), :] = turned.astype(jnp.bfloat16)
        base += width
    for b in range(owned):
        for part in range(hidden // width):
            piece = contract_last(order, w3[b, pl.ds(part * width, width), :])
            packed[pl.ds(base, width), :] = piece.astype(jnp.bfloat16)
            base += width
    for a in range(owned):
        packed[pl.ds(base, width), :] = contract_last(order, w1[a]).astype(jnp.bfloat16)
        base += width


def start_loading(gathered, second, fourth, third, first, sems):
    owned, width, hidden = third.shape[1:]
    groups = []
    base = 0
    for target, length in ((second, hidden), (fourth, width)):
        group = []
        for half in range(owned):
            group.append((gathered.at[:, pl.ds(base, length), :], target.at[:, half]))
            base += length
        groups.append(group)
    group = []
    for half in range(owned):
        for part in range(hidden // width):
            place = third.at[:, half, :, pl.ds(part * width, width)]
            group.append((gathered.at[:, pl.ds(base, width), :], place))
            base += width
    groups.append(group)
    group = []
    for half in range(owned):
        group.append((gathered.at[:, pl.ds(base, width), :], first.at[:, half]))
        base += width
    groups.append(group)
    started = []
    number = 0
    for group in groups:
        copies = []
        for source, target in group:
            copy = pltpu.make_async_copy(source, target, sems.at[number])
            copy.start()
            copies.append(copy)
            number += 1
        started.append(copies)
    return started


def wait_all(copies):
    for copy in copies:
        copy.wait()


def first_body(
    turn,
    section,
    by_rows,
    gathered,
    result,
    kept,
    slope,
    second,
    fourth,
    third,
    first,
    rows_in,
    rows_out,
    grad_lin,
    sems,
):
    blocks, _, rows, width = by_rows.shape
    owned = third.shape[1]
    to_second, to_fourth, to_third, to_first = start_loading(
        gathered, second, fourth, third, first, sems
    )
    rows_in[...] = by_rows[:, 0].astype(jnp.float32).reshape(blocks * rows, width)
    exchange_blocks(rows_in, rows_out, blocks, rows)
    wait_all(to_second)
    for b in range(blocks):
        mixed = rows_out[pl.ds(b * rows, rows), :].astype(jnp.bfloat16)
        slope[b] = gelu_slope(contract_last(mixed, second[b // owned, b % owned]))
    wait_all(to_fourth)
    wait_all(to_third)
    wait_all(to_first)

    @pl.when(section[0] != turn)
    def _():
        result[...] = by_rows[:, 1]
        for kind in range(kept.shape[1]):
            kept[:, kind] = by_rows[:, 1]

    @pl.when(section[0] == turn)
    def _():
        result[...] = by_rows[:, 1]
        one_section(
            result, kept, slope, second, fourth, third, first, rows_in, rows_out, grad_lin
        )


def one_section(result, kept, slope, second, fourth, third, first, rows_in, rows_out, grad_lin):
    blocks, rows, width = result.shape
    owned = third.shape[1]
    kept[:, 0] = result[...]
    for a in range(blocks):
        rows_in[pl.ds(a * rows, rows), :] = jnp.dot(
            kept[a, 0], fourth[a // owned, a % owned], preferred_element_type=jnp.float32
        )
    exchange_blocks(rows_in, rows_out, blocks, rows)
    kept[:, 1] = rows_out[...].reshape(blocks, rows, width).astype(jnp.bfloat16)
    for b in range(blocks):
        grad_hid = jnp.dot(
            kept[b, 1], third[b // owned, b % owned], preferred_element_type=jnp.float32
        )
        grad_lin[b] = (grad_hid * slope[b]).astype(jnp.bfloat16)
    for b in range(blocks):
        rows_in[pl.ds(b * rows, rows), :] = jnp.dot(
            grad_lin[b], second[b // owned, b % owned], preferred_element_type=jnp.float32
        )
    exchange_blocks(rows_in, rows_out, blocks, rows)
    kept[:, 2] = rows_out[...].reshape(blocks, rows, width).astype(jnp.bfloat16)
    for a in range(blocks):
        term = jnp.dot(
            kept[a, 2], first[a // owned, a % owned], preferred_element_type=jnp.float32
        )
        result[a] = (kept[a, 0].astype(jnp.float32) + term).astype(jnp.bfloat16)


def step_body(
    turn,
    section,
    cotangent,
    old_kept,
    slope,
    second,
    fourth,
    third,
    first,
    result,
    kept,
    rows_in,
    rows_out,
    grad_lin,
):
    result[...] = cotangent[...]

    @pl.when(section[0] != turn)
    def _():
        kept[...] = old_kept[...]

    @pl.when(section[0] == turn)
    def _():
        one_section(
            result, kept, slope, second, fourth, third, first, rows_in, rows_out, grad_lin
        )


def reload_body(gathered, second, fourth, third, first, sems):
    for copies in start_loading(gathered, second, fourth, third, first, sems):
        wait_all(copies)


def gradients_body(
    returned,
    w1,
    w3,
    inputs,
    mixed,
    gelu_rows,
    slope,
    handed_back,
    grad_inputs,
    grad_w1,
    grad_w2,
    grad_w3,
    grad_w4,
):
    devices, owned, _, rows, width = returned.shape
    order = order_matrix(width, devices * owned, width // (devices * owned))

    def rows_of(block, kind):
        value = returned[:, block, kind].astype(jnp.float32)
        return value.reshape(devices * rows, width)

    def in_natural_order(value):
        return jnp.dot(
            value.astype(jnp.bfloat16), order, preferred_element_type=jnp.float32
        ).astype(jnp.bfloat16)

    for a in range(owned):
        gy = rows_of(a, 0)
        gu = in_natural_order(rows_of(a, 2))
        grad_inputs[:, a * width : (a + 1) * width] = (gy + contract_last(gu, w1[a])).astype(
            jnp.bfloat16
        )
        grad_w1[a] = jnp.dot(inputs[a], gu, preferred_element_type=jnp.float32)
        grad_w4[a] = jnp.dot(
            handed_back[a], gy.astype(jnp.bfloat16), preferred_element_type=jnp.float32
        )
    for b in range(owned):
        gv = in_natural_order(rows_of(b, 1))
        grad_lin = (contract_last(w3[b], gv) * slope[b]).astype(jnp.bfloat16)
        grad_w2[b] = contract_last(mixed[b], grad_lin)
        grad_w3[b] = jnp.dot(gelu_rows[b], gv, preferred_element_type=jnp.float32)


def in_vmem(count):
    return [IN_VMEM] * count


def to_owners(value):
    return lax.all_to_all(value, "tensor", split_axis=0, concat_axis=0, tiled=True)


def tied(value, anchor):
    return lax.optimization_barrier((value, anchor))[0]


def local(section_inputs, out_grad, w1, w2, w3, w4):
    devices = lax.axis_size("tensor")
    section_count = lax.axis_size("section")
    section = lax.axis_index("section").astype(jnp.int32).reshape(1)
    all_rows = section_inputs.shape[1] * section_inputs.shape[2]
    owned, width, hidden = w2.shape[1:]
    blocks = owned * devices
    spread = width // blocks
    rows = all_rows // devices
    packed_rows = owned * (2 * hidden + 2 * width)
    bf16, f32 = jnp.bfloat16, jnp.float32

    packed = pl.pallas_call(
        functools.partial(prepare_body, blocks),
        out_shape=jax.ShapeDtypeStruct((packed_rows, width), bf16),
        in_specs=in_vmem(4),
        out_specs=IN_VMEM,
        compiler_params=pltpu.CompilerParams(vmem_limit_bytes=16 * MIB),
        name="prepare_weights",
    )(w1[0], w2[0], w3[0], w4[0])
    gathered = lax.all_gather(packed, "tensor", axis=0, tiled=False)

    input_rows = section_inputs[0].reshape(all_rows, owned, width)
    first_local = packed[packed_rows - owned * width :].reshape(owned, width, width)
    raised = matrix_product("tac,apc->atp", input_rows, first_local).astype(bf16)
    raised = raised.reshape(owned, devices, rows, width).transpose(1, 0, 2, 3)
    targets = out_grad.reshape(devices, rows, owned, width).transpose(0, 2, 1, 3)
    by_rows = to_owners(jnp.stack([raised, targets], axis=2))
    by_rows = by_rows.reshape(blocks, 2, rows, width)

    def forward(input_rows, w1, w2, w3):
        raised_rows = matrix_product("owz,wzy->wyo", input_rows, w1).astype(bf16)
        mixed = lax.all_to_all(raised_rows, "tensor", split_axis=1, concat_axis=0, tiled=True)
        mixed = mixed.reshape(blocks, owned, spread, all_rows).transpose(1, 0, 2, 3)
        mixed = mixed.reshape(owned, width, all_rows)
        linear = matrix_product("bkt,bkn->bnt", mixed, w2)
        gelu_rows = gelu_tanh(linear).astype(bf16)
        slope = gelu_slope(linear)
        lowered = matrix_product("bnt,bnk->bkt", gelu_rows, w3).astype(bf16)
        back = lax.all_to_all(lowered, "tensor", split_axis=1, concat_axis=0, tiled=True)
        back = back.reshape(blocks, owned, spread, all_rows).transpose(1, 0, 2, 3)
        back = back.reshape(owned, width, all_rows)
        return input_rows.transpose(1, 2, 0), mixed, gelu_rows, slope, back

    weight_shapes = [
        pltpu.VMEM((devices, owned, hidden, width), bf16),
        pltpu.VMEM((devices, owned, width, width), bf16),
        pltpu.VMEM((devices, owned, width, hidden), bf16),
        pltpu.VMEM((devices, owned, width, width), bf16),
    ]
    copies = pltpu.SemaphoreType.DMA((owned * (3 + hidden // width),))
    row_shape = jax.ShapeDtypeStruct((blocks, rows, width), bf16)
    kept_shape = jax.ShapeDtypeStruct((blocks, 3, rows, width), bf16)
    scratch = [
        pltpu.VMEM((blocks * rows, width), f32),
        pltpu.VMEM((blocks * rows, width), f32),
        pltpu.VMEM((blocks, rows, hidden), bf16),
    ]
    last = section_count - 1
    cotangent, kept, slope, *weights = pl.pallas_call(
        functools.partial(first_body, last),
        out_shape=[row_shape, kept_shape, pltpu.VMEM((blocks, rows, hidden), f32)]
        + weight_shapes,
        in_specs=[IN_SMEM, IN_VMEM, IN_PLACE],
        out_specs=in_vmem(7),
        scratch_shapes=scratch + [copies],
        compiler_params=pltpu.CompilerParams(vmem_limit_bytes=36 * MIB),
        name="load_and_first_section",
    )(section, by_rows, gathered)
    forward_values = None
    for turn in range(last, -1, -1):
        if turn < last:
            cotangent = lax.ppermute(cotangent, "section", [(turn + 1, turn)])
            cotangent, kept = pl.pallas_call(
                functools.partial(step_body, turn),
                out_shape=[row_shape, kept_shape],
                in_specs=[IN_SMEM] + in_vmem(7),
                out_specs=in_vmem(2),
                scratch_shapes=scratch,
                compiler_params=pltpu.CompilerParams(vmem_limit_bytes=8 * MIB),
                name="section_step",
            )(section, cotangent, kept, slope, *weights)
        if turn == section_count // 2:
            given = tied((input_rows, w1[0], w2[0], w3[0]), kept)
            forward_values = forward(*given)
            gathered = tied(gathered, forward_values)
            weights = pl.pallas_call(
                reload_body,
                out_shape=weight_shapes,
                in_specs=[IN_PLACE],
                out_specs=in_vmem(4),
                scratch_shapes=[copies],
                compiler_params=pltpu.CompilerParams(vmem_limit_bytes=36 * MIB),
                name="load_again",
            )(gathered)

    returned = to_owners(kept.reshape(devices, owned, 3, rows, width))
    grad_inputs, *grads = pl.pallas_call(
        gradients_body,
        out_shape=[
            jax.ShapeDtypeStruct((all_rows, owned * width), bf16),
            jax.ShapeDtypeStruct((owned, width, width), f32),
            jax.ShapeDtypeStruct((owned, width, hidden), f32),
            jax.ShapeDtypeStruct((owned, hidden, width), f32),
            jax.ShapeDtypeStruct((owned, width, width), f32),
        ],
        in_specs=in_vmem(8),
        out_specs=in_vmem(5),
        compiler_params=pltpu.CompilerParams(vmem_limit_bytes=24 * MIB),
        name="gradients",
    )(returned, w1[0], w3[0], *forward_values)
    grad_inputs = grad_inputs.reshape(section_inputs.shape)
    return (grad_inputs, *[grad[None] for grad in grads])


def solution(mesh):
    in_specs = (
        P("section", None, None, "tensor"),
        P(None, None, "tensor"),
        P("section", "tensor", None, None),
        P("section", "tensor", None, None),
        P("section", "tensor", None, None),
        P("section", "tensor", None, None),
    )
    out_specs = (
        P("section", None, None, "tensor"),
        P("section", "tensor", None, None),
        P("section", "tensor", None, None),
        P("section", "tensor", None, None),
        P("section", "tensor", None, None),
    )
    return jax.shard_map(local, mesh=mesh, in_specs=in_specs, out_specs=out_specs, check_vma=False)
```

time: 1010 us -> 412 us (0.41)
  waiting for transfers between devices: 583 us -> 233 us
  starting transfers between devices: 211 us -> 32.7 us
  matrix products: 115 us -> 1.55 us
  blocking collectives: 0 us -> 71.6 us
  local copies, waits for them, and re-layouts: 67.5 us -> 14.5 us
  Pallas kernels: 0 us -> 35.5 us
  other arithmetic: 17.3 us -> 0.03 us
  between operations: 1.03 us -> 15 us
    all_to_all x34 -> x2, waiting for transfers between devices: 517 us -> 39.5 us  [the longest x1 24.2 us: to_owners(): lax.all_to_all(value, 'tensor', split_axis=0, concat_axis=0, tiled=True)]
    all_to_all x34 -> x2, starting transfers between devices: 191 us -> 21.9 us  [the longest x1 16.7 us: to_owners(): lax.all_to_all(value, 'tensor', split_axis=0, concat_axis=0, tiled=True)]
    dot_general x131 -> x4, matrix products: 115 us -> 1.55 us  [matrix_product(): jnp.einsum(form, left_side, right_side, preferred_element_type=jnp.float32)]
    all_gather x0 -> x1, waiting for transfers between devices: none -> 97.7 us  [local(): gathered = lax.all_gather(packed, 'tensor', axis=0, tiled=False)]
    all_to_all x0 -> x2, blocking collectives: none -> 71.6 us  [the longest x1 46.3 us: to_owners(): lax.all_to_all(value, 'tensor', split_axis=0, concat_axis=0, tiled=True)]
    pallas_call x0 -> x19, Pallas kernels: none -> 35.5 us  [the longest x15 15.7 us: local(): pl.pallas_call(functools.partial(step_body, turn), out_shape=[row_shape,...]
    ppermute x15, waiting for transfers between devices: 66.3 us -> 96.1 us  [local(): cotangent = lax.ppermute(cotangent, 'section', [(turn + 1, turn)])]
    reshape x37 -> x5, local copies, waits for them, and re-layouts: 25.2 us -> 2.96 us  [the longest x1 0.96 us: forward(): back = back.reshape(owned, width, all_rows)]
  transfers between devices with their start and end apart: 49 -> 18, of which waited for: 49 -> 4; matrix products, arithmetic and copies ran while one was open for 6% -> 2% of each run, Pallas kernels for 0% -> 2%
where the time goes in v2:
time: 412 us; the launch traced here: 404 us
  waiting for transfers between devices  233 us (57%)
  blocking collectives  71.6 us (17%)
  Pallas kernels  35.5 us (9%)
  starting transfers between devices  32.7 us (8%)
  between operations  15 us (4%)
  local copies, waits for them, and re-layouts  14.5 us (4%)
    all_gather x1, waiting for transfers between devices, local(): gathered = lax.all_gather(packed, 'tensor', axis=0, tiled=False)  97.7 us
    ppermute x15, waiting for transfers between devices, local(): cotangent = lax.ppermute(cotangent, 'section', [(turn + 1, turn)])  96.1 us
    all_to_all x1, blocking collectives, to_owners(): lax.all_to_all(value, 'tensor', split_axis=0, concat_axis=0, tiled=True)  46.3 us
    all_to_all x1, blocking collectives, forward(): lax.all_to_all(raised_rows, 'tensor', split_axis=1, concat_axis=0, tiled=...  25.3 us
    all_to_all x1, waiting for transfers between devices, to_owners(): lax.all_to_all(value, 'tensor', split_axis=0, concat_axis=0, tiled=True)  24.2 us
    all_to_all x1, starting transfers between devices, to_owners(): lax.all_to_all(value, 'tensor', split_axis=0, concat_axis=0, tiled=True)  16.7 us
    pallas_call x15, Pallas kernels, local(): pl.pallas_call(functools.partial(step_body, turn), out_shape=[row_shape,...  15.7 us
    all_to_all x1, waiting for transfers between devices, forward(): lax.all_to_all(lowered, 'tensor', split_axis=1, concat_axis=0, tiled=True)  15.3 us
  transfers between devices with their start and end apart: 18, of which 4 were waited for; matrix products, arithmetic and copies ran while one was open for 2% of the time, Pallas kernels for 2%

profile of v2, /device:TPU:1, one launch (start us, length us, event | category | flops | bytes accessed | tf_op | source)
XLA Modules:
  0.0 404.3 jit_solution(9473673554570059941)
XLA Ops:
  7.2 0.9 copy-done
  8.2 0.8 copy-done.2
  9.0 0.9 copy-done.7
  10.0 0.8 copy-done.9
  10.8 1.3 prepare_weights.1
  12.1 0.8 slice.4
  13.0 0.9 reshape.57
  14.0 0.9 copy.72
  15.3 0.7 copy.47
  16.0 16.7 %all-to-all-start = ((bf16[32,2,2,8,128]{4,3,1,2,0:T(8,128)(2,1)}), bf16[32,2,2,8,128]{4,3,1,2,0:T(8,128)(2,1)S(1)}, u32[]{:S(2)}, u32[]{:S(2)}) async-start(bf16[32,2,2,8,128]{4,3,1,2,0:T(8,128)(2,1)} %copy.47), calls=%async_computation | async-start | bytes 524288 | tf_op jit(solution)/shard_map/all_to_all | solution.py:276
  32.8 24.2 %all-to-all-done = bf16[32,2,2,8,128]{4,3,1,2,0:T(8,128)(2,1)S(1)} async-done(((bf16[32,2,2,8,128]{4,3,1,2,0:T(8,128)(2,1)}), bf16[32,2,2,8,128]{4,3,1,2,0:T(8,128)(2,1)S(1)}, u32[]{:S(2)}, u32[]{:S(2)}) %all-to-all-start) | async-done | bytes 262176 | tf_op jit(solution)/shard_map/all_to_all | solution.py:276
  57.7 97.7 %all-gather.3.cloned.1.call-done = bf16[81920,128]{1,0:T(8,128)(2,1)} async-done(((bf16[2560,128]{1,0:T(8,128)(2,1)}), bf16[81920,128]{1,0:T(8,128)(2,1)}) %all-gather.3.cloned.1.call-update) | async-done | bytes 20971536 | tf_op jit(solution)/shard_map/all_gather | solution.py:303
  155.4 8.9 %load_and_first_section.1 = (bf16[64,8,128]{2,1,0:T(8,128)(2,1)}, bf16[64,3,8,128]{3,2,1,0:T(8,128)(2,1)}, f32[64,8,512]{2,1,0:T(8,128)S(1)}, bf16[32,2,512,128]...) custom-call(s32[1]{0:T(128)} %bitcast.section, ...), custom_call_target="tpu_custom_call" | custom-call | tf_op jit(solution)/shard_map/load_and_first_section/pallas_call | solution.py:342
  165.0 1.0 copy-done.6
  169.2 6.4 %section_step.19 = (bf16[64,8,128]{2,1,0:T(8,128)(2,1)S(1)}, bf16[64,3,8,128]{3,2,1,0:T(8,128)(2,1)S(1)}) custom-call(s32[1]{0:T(128)} %bitcast.section, bf16[64,8,128]{2,1,0:T(8,128)(2,1)S(1)} %collective-permute-done.4.cotangent, bf16[64,3,8,128]{3,2,1,0:T(8,128)(2,1)S(1)} %get-tuple-element.69.old_kept, f32[64,8,512]{2,1,0:T(8,128)S(1)} %get-tuple-element.57.slope, ...), custom_call_target="tpu_custom_call" | custom-call | tf_op jit(solution)/shard_map/section_step/pallas_call | solution.py:356
  178.2 25.3 %all_to_all.40 = bf16[2,128,256]{2,0,1:T(2,128)(2,1)S(1)} all-to-all(bf16[2,128,256]{2,0,1:T(2,128)(2,1)S(1)} %copy.51), channel_id=1, replica_groups=mesh['section'=16,'tensor'=32] {'tensor'}, dimensions={1} | all-to-all | bytes 262144 | tf_op jit(solution)/shard_map/all_to_all | solution.py:315
  203.9 0.9 fusion.5
  205.1 0.8 copy.56
  205.9 5.1 %all-to-all-start.2 = ((bf16[2,128,256]{2,0,1:T(2,128)(2,1)}), bf16[2,128,256]{2,0,1:T(2,128)(2,1)S(1)}, u32[]{:S(2)}, u32[]{:S(2)}) async-start(bf16[2,128,256]{2,0,1:T(2,128)(2,1)} %copy.56), calls=%async_computation.2 | async-start | bytes 262144 | tf_op jit(solution)/shard_map/all_to_all | solution.py:322
  211.0 0.8 collective-permute-start.7
  211.9 15.3 %all-to-all-done.2 = bf16[2,128,256]{2,0,1:T(2,128)(2,1)S(1)} async-done(((bf16[2,128,256]{2,0,1:T(2,128)(2,1)}), bf16[2,128,256]{2,0,1:T(2,128)(2,1)S(1)}, u32[]{:S(2)}, u32[]{:S(2)}) %all-to-all-start.2) | async-done | bytes 131104 | tf_op jit(solution)/shard_map/all_to_all | solution.py:322
  227.2 0.7 copy.70
  228.0 1.0 reshape.52
  228.9 0.8 copy.58
  229.7 1.0 reshape.53.handed_back
  230.7 7.2 %load_again.1 = (bf16[32,2,512,128]{3,2,1,0:T(8,128)(2,1)S(1)}, bf16[32,2,128,128]{3,2,1,0:T(8,128)(2,1)S(1)}, bf16[32,2,128,512]{3,2,1,0:T(8,128)(2,1)S(1)}, bf16[32,2,128,128]{3,2,1,0:T(8,128)(2,1)S(1)}) custom-call(bf16[32,2560,128]{2,1,0:T(8,128)(2,1)} %bitcast.64), custom_call_target="tpu_custom_call" | custom-call | tf_op jit(solution)/shard_map/load_again/pallas_call | solution.py:369
  242.5 3.5 section_step.28
  246.1 1.3 collective-permute-start.14
  247.4 96.1 %collective-permute-done.14.cotangent = bf16[64,8,128]{2,1,0:T(8,128)(2,1)S(1)} collective-permute-done((bf16[64,8,128]{2,1,0:T(8,128)(2,1)S(1)}, bf16[64,8,128]{2,1,0:T(8,128)(2,1)S(1)}, u32[]{:S(2)}, u32[]{:S(2)}) %collective-permute-start.14) | collective-permute-done | bytes 131104 | tf_op jit(solution)/shard_map/ppermute | solution.py:355
  343.4 4.8 %section_step.29 = (bf16[64,8,128]{2,1,0:T(8,128)(2,1)}, bf16[64,3,8,128]{3,2,1,0:T(8,128)(2,1)S(1)}) custom-call(s32[1]{0:T(128)} %bitcast.section, bf16[64,8,128]{2,1,0:T(8,128)(2,1)S(1)} %collective-permute-done.14.cotangent, bf16[64,3,8,128]{3,2,1,0:T(8,128)(2,1)S(1)} %get-tuple-element.98.old_kept, f32[64,8,512]{2,1,0:T(8,128)S(1)} %get-tuple-element.57.slope, ...), custom_call_target="tpu_custom_call" | custom-call | tf_op jit(solution)/shard_map/section_step/pallas_call | solution.py:356
  348.2 46.3 %all_to_all.41.returned = bf16[32,2,3,8,128]{4,3,2,1,0:T(8,128)(2,1)S(1)} all-to-all(bf16[32,2,3,8,128]{4,3,2,1,0:T(8,128)(2,1)S(1)} %bitcast.59), channel_id=1, replica_groups=mesh['section'=16,'tensor'=32] {'tensor'}, dimensions={0} | all-to-all | bytes 786432 | tf_op jit(solution)/shard_map/all_to_all | solution.py:276
  394.6 2.4 gradients.1
  (70 shorter events, 12.7 us)
Async XLA Ops:
  7.2 148.2 %all-gather.3.cloned.1.call-start = ((), (), s32[]{:S(2)}) async-start(), calls=%async_computation.4 | async-start | bytes 21626880 | tf_op jit(solution)/shard_map/all_gather | solution.py:303
  7.2 1.0 copy-start
  8.2 0.8 copy-start.2
  9.0 0.9 copy-start.7
  10.0 0.8 copy-start.9
  16.0 40.9 %all-to-all-start = ((bf16[32,2,2,8,128]{4,3,1,2,0:T(8,128)(2,1)}), bf16[32,2,2,8,128]{4,3,1,2,0:T(8,128)(2,1)S(1)}, u32[]{:S(2)}, u32[]{:S(2)}) async-start(bf16[32,2,2,8,128]{4,3,1,2,0:T(8,128)(2,1)} %copy.47), calls=%async_computation | async-start | bytes 524288 | tf_op jit(solution)/shard_map/all_to_all | solution.py:276
  164.3 0.7 collective-permute-start
  165.0 1.0 copy-start.6
  166.0 0.7 collective-permute-start.1
  167.0 0.7 collective-permute-start.2
  167.7 0.7 collective-permute-start.3
  168.5 0.7 collective-permute-start.4
  175.6 0.7 collective-permute-start.5
  176.3 0.7 collective-permute-start.6
  177.0 0.8 copy-start.3
  177.0 26.9 %copy-start.8 = (bf16[1,2,128,512]{3,2,1,0:T(8,128)(2,1)S(1)}, bf16[1,2,128,512]{3,2,1,0:T(8,128)(2,1)}, u32[]{:S(2)}) copy-start(bf16[1,2,128,512]{3,2,1,0:T(8,128)(2,1)} %param.9) | copy-start | bytes 786436
  177.1 0.7 copy-start.4
  177.8 26.0 %copy-start.10 = (bf16[64,8,128]{2,1,0:T(8,128)(2,1)}, bf16[64,8,128]{2,1,0:T(8,128)(2,1)S(1)}, u32[]{:S(2)}) copy-start(bf16[64,8,128]{2,1,0:T(8,128)(2,1)S(1)} %get-tuple-element.74) | copy-start | bytes 393220
  177.8 27.0 %copy-start.1 = (bf16[1,2,512,128]{3,2,1,0:T(8,128)(2,1)S(1)}, bf16[1,2,512,128]{3,2,1,0:T(8,128)(2,1)}, u32[]{:S(2)}) copy-start(bf16[1,2,512,128]{3,2,1,0:T(8,128)(2,1)} %param.10) | copy-start | bytes 786436
  205.9 21.3 %all-to-all-start.2 = ((bf16[2,128,256]{2,0,1:T(2,128)(2,1)}), bf16[2,128,256]{2,0,1:T(2,128)(2,1)S(1)}, u32[]{:S(2)}, u32[]{:S(2)}) async-start(bf16[2,128,256]{2,0,1:T(2,128)(2,1)} %copy.56), calls=%async_computation.2 | async-start | bytes 262144 | tf_op jit(solution)/shard_map/all_to_all | solution.py:322
  211.0 26.8 %collective-permute-start.7 = (bf16[64,8,128]{2,1,0:T(8,128)(2,1)}, bf16[64,8,128]{2,1,0:T(8,128)(2,1)S(1)}, u32[]{:S(2)}, u32[]{:S(2)}) collective-permute-start(bf16[64,8,128]{2,1,0:T(8,128)(2,1)} %copy-done.10), channel_id=1, source_target_pairs={{256,224},{257,225},{258,226},{259,227},{260,228},{261,229},{262,2... | collective-permute-start | bytes 393224 | tf_op jit(solution)/shard_map/ppermute | solution.py:355
  230.7 7.2 %copy-start.5 = (bf16[64,3,8,128]{3,2,1,0:T(8,128)(2,1)S(1)}, bf16[64,3,8,128]{3,2,1,0:T(8,128)(2,1)}, u32[]{:S(2)}) copy-start(bf16[64,3,8,128]{3,2,1,0:T(8,128)(2,1)} %copy-done.4) | copy-start | bytes 1179652
  237.9 0.7 collective-permute-start.8
  238.7 0.7 collective-permute-start.9
  239.4 0.7 collective-permute-start.10
  240.4 0.7 collective-permute-start.11
  241.1 0.7 collective-permute-start.12
  241.9 0.7 collective-permute-start.13
  246.1 97.4 %collective-permute-start.14 = (bf16[64,8,128]{2,1,0:T(8,128)(2,1)S(1)}, bf16[64,8,128]{2,1,0:T(8,128)(2,1)S(1)}, u32[]{:S(2)}, u32[]{:S(2)}) collective-permute-start(bf16[64,8,128]{2,1,0:T(8,128)(2,1)S(1)} %get-tuple-element.97), channel_id=1, source_target_pairs={{32,0},{33,1},{34,2},{35,3},{36,4},{37,5},{38,6},{39,7},{40,8},{41... | collective-permute-start | bytes 393224 | tf_op jit(solution)/shard_map/ppermute | solution.py:355
Sparse Core Ops, SparseCore 0:
  12.2 143.0 all-gather.2
